TPU v7x, 32 devices: a whole 2x2x4 slice. The times are simulated.
32 devices in a mesh: section: 2 (over x), ctx: 16 (over z, y, core).
Axes of the slice: x: 2, y: 2, z: 4, core: 2. Of those that a mesh axis runs over, the one named last changes fastest.
Arguments:
- activations: bfloat16 [2, 24, 8192], P('section'), may hold values from -6 to 6
- act_frames: int32 [2, 24], replicated, may hold values from 0 to 191
- fresh_batch: bfloat16 [24, 8192], replicated, may hold values from -6 to 6
- fresh_frames: int32 [24], replicated, may hold values from 0 to 191
- norm_gain: float32 [2, 8192], P('section'), may hold values from 0.1 to 1.9
- cached_keys: bfloat16 [2, 12288, 1024], P('section', 'ctx'), may hold values from -64 to 64
- cached_values: bfloat16 [2, 12288, 1024], P('section', 'ctx'), may hold values from -6 to 6
- key_frames: int32 [12288], P('ctx'), may hold values from 0 to 191, never falling along the last dimension, each value on 1 to 128 neighbouring positions
Outputs:
- result: bfloat16 [2, 24, 8192], P('section')
Inputs may be any that keep to these rules, and one draw needn't show every extreme that they name: `key_frames`: frame indices never fall along the clip, and every frame of 0 to 191 holds at least one token.
All inputs are finite; a program needn't handle non-finite values.
Results may differ from a plain program's by a relative error of at most 0.019.
Values may be sent and summed in bfloat16 or wider, within the bound.
No kernel may reach another device: no remote copies, remote signals or barrier semaphores. Data moves between devices by JAX's collectives and lax.ppermute only.
A program may use at most 64 MiB of HBM per device.

v0:
```python
import functools
import math

import jax
import jax.numpy as jnp
from jax import lax
from jax.experimental import pallas as pl
from jax.experimental.pallas import tpu as pltpu
from jax.sharding import PartitionSpec as P

HEADS = 64
HD = 128
PAIR = 2
INNER = 2
BLOCKS = 4
STAT_ROWS = 16
HIDDEN = -(2.0**100)
SCALE = HD**-0.5 * math.log2(math.e)
MIB = 1 << 20

epsilon = 1e-05

WHOLE = pl.BlockSpec(memory_space=pltpu.VMEM)
IN_HBM = pl.BlockSpec(memory_space=pltpu.HBM)


def in_hbm(*arrays):
    return [pltpu.with_memory_space_constraint(a, pltpu.HBM) for a in arrays]


def in_vmem(*arrays):
    return [pltpu.with_memory_space_constraint(a, pltpu.VMEM) for a in arrays]


def place_here():
    return lax.axis_index("ctx") % PAIR


def inner_here():
    return lax.axis_index("ctx") // PAIR % INNER


def outer_here():
    return lax.axis_index("ctx") // (PAIR * INNER)


def in_first_section():
    return lax.axis_index("section") == 0


def swapped(block):
    return lax.ppermute(block, "ctx", [(i, i ^ 1) for i in range(lax.axis_size("ctx"))])


def from_inner(block):
    size = lax.axis_size("ctx")
    return lax.ppermute(block, "ctx", [(i, i ^ PAIR ^ 1) for i in range(size)])


def from_outer(blocks, other_place=1):
    size = lax.axis_size("ctx")
    got = [
        lax.ppermute(
            block, "ctx", [(i, i ^ (INNER * PAIR * d) ^ other_place) for i in range(size)]
        )
        for d, block in reversed(list(enumerate(blocks, 1)))
    ]
    return got[::-1]


def from_section_before(block, step):
    sections, size = lax.axis_size("section"), lax.axis_size("ctx")
    route = [
        (s * size + i, (s + 1) % sections * size + (i ^ (PAIR * step) ^ 1))
        for s in range(sections)
        for i in range(size)
    ]
    return lax.ppermute(block, ("section", "ctx"), route)


def head_rows(block):
    return jnp.concatenate(
        [block[:, at : at + HD] for at in range(0, block.shape[1], HD)], axis=0
    )


def row_of(ref):
    return jnp.concatenate([ref[i : i + 1] for i in range(ref.shape[0])], axis=1)


def columns_of(index, ref, width):
    return ref.at[:, pl.ds(pl.multiple_of(index * width, HD), width)]


def on_diagonal(rows):
    shape = (rows, HD)
    return lax.broadcasted_iota(jnp.int32, shape, 0) == lax.broadcasted_iota(jnp.int32, shape, 1)


def queries_of(x, gain):
    rows = head_rows(x.astype(jnp.float32))
    gain = head_rows(jnp.broadcast_to(gain, x.shape))
    norm = lax.rsqrt(jnp.mean(rows * rows, axis=-1, keepdims=True) + epsilon)
    return (rows * norm * gain).astype(jnp.bfloat16)


def bias_of(keys_ref, frames):
    length = keys_ref.shape[0] - STAT_ROWS
    width = keys_ref.shape[1]
    rows = -(-length // width)
    tail = keys_ref[length:].astype(jnp.float32)
    key_frames = jnp.concatenate([tail[i : i + 1] for i in range(rows)], axis=1)[:, :length]
    return jnp.where(key_frames <= frames, 0.0, HIDDEN)[None]


def scores(queries, key_block, bias):
    count, keys, tokens = queries.shape[0], key_block.shape[0], bias.shape[1]
    raw = lax.dot_general(
        queries, key_block, (((1,), (1,)), ((), ())), preferred_element_type=jnp.float32
    )
    raw = raw.reshape(count // tokens, tokens, keys) * SCALE + bias
    return raw.reshape(count, keys)


def top_of(raw):
    top = jnp.max(raw, axis=-1, keepdims=True)
    return top.astype(jnp.bfloat16).astype(jnp.float32)


def weigh(raw, top, value_block):
    probs = jnp.exp2(raw - top).astype(jnp.bfloat16)
    ones = jnp.ones((value_block.shape[0], HD), jnp.bfloat16)
    return jnp.dot(
        probs, jnp.concatenate([value_block, ones], axis=1), preferred_element_type=jnp.float32
    )


def groups_of(count):
    groups = -(-count // HD)
    held = count // groups
    return [slice(c * held, (c + 1) * held) for c in range(groups)]


def write_chunk(out_ref, weighted, tops, totals):
    count = weighted.shape[0]
    line = lax.broadcasted_iota(jnp.int32, (STAT_ROWS, HD), 0)
    stats = jnp.zeros((STAT_ROWS, HD), jnp.float32)
    for c, (top, total) in enumerate(zip(tops, totals)):
        high = total.astype(jnp.bfloat16).astype(jnp.float32)
        for n, row in enumerate((top, high, total - high)):
            stats = jnp.where(line == 3 * c + n, row, stats)
    out_ref[:count] = weighted.astype(jnp.bfloat16)
    out_ref[count:] = stats.astype(jnp.bfloat16)


def write_sums(out_ref, weighted, top, total):
    groups = groups_of(weighted.shape[0])
    diagonal = on_diagonal(groups[0].stop)

    def rows(column):
        column = jnp.broadcast_to(column, weighted.shape)
        return [
            jnp.sum(jnp.where(diagonal, column[group], 0.0), axis=0, keepdims=True)
            for group in groups
        ]

    write_chunk(out_ref, weighted, rows(top), rows(total))


def joined(parts, normed, x=None):
    count = parts[0].shape[0] - STAT_ROWS
    groups = groups_of(count)
    diagonal = on_diagonal(groups[0].stop)
    stats = [part[count:].astype(jnp.float32) for part in parts]
    values, tops, totals = [], [], []
    for c, group in enumerate(groups):
        points = [s[3 * c : 3 * c + 1] for s in stats]
        top = functools.reduce(jnp.maximum, points)
        factors = [jnp.exp2(point - top) for point in points]
        total = sum(
            f * (s[3 * c + 1 : 3 * c + 2] + s[3 * c + 2 : 3 * c + 3])
            for f, s in zip(factors, stats)
        )
        if normed:
            inverse = 1.0 / total
            factors = [f * inverse for f in factors]
        terms = list(zip(factors, parts)) + ([] if x is None else [(total, x)])
        value = 0.0
        for factor, part in terms:
            weight = jnp.where(diagonal, factor, 0.0)[:, : group.stop - group.start]
            high = weight.astype(jnp.bfloat16)
            low = (weight - high.astype(jnp.float32)).astype(jnp.bfloat16)
            for term in (high, low):
                value = value + jnp.dot(term, part[group], preferred_element_type=jnp.float32)
        values.append(value)
        tops.append(top)
        totals.append(total)
    return jnp.concatenate(values, axis=0), tops, totals


def halve(staged_ref, copies, own_ref, given_ref):
    length, width = staged_ref.shape
    half, step = width // PAIR, length // BLOCKS
    place = place_here()
    for b in range(BLOCKS):
        if copies:
            copies[b].wait()
        rows = pl.ds(b * step, step)
        given_ref[rows] = columns_of(1 - place, staged_ref.at[rows], half)[...]
        own_ref[rows] = columns_of(place, staged_ref.at[rows], half)[...]


def column_of(row):
    shape = (row.shape[1], row.shape[1])
    diagonal = lax.broadcasted_iota(jnp.int32, shape, 0) == lax.broadcasted_iota(jnp.int32, shape, 1)
    return jnp.sum(jnp.where(diagonal, row, 0.0), axis=1, keepdims=True)


def load_keys_kernel(
    act_frames_in, fresh_frames_in, key_frames_in, batch_in, fresh_in, gain_in, keys_in,
    own_ref, given_ref, batch_ref, gain_ref, share_ref, fresh_ref, fresh_gain_ref, frames_ref,
    act_frames_ref, fresh_frames_ref, key_frames_ref, staged_ref, sems, small_sems,
):
    place, length, width = place_here(), staged_ref.shape[0], own_ref.shape[1]
    share = fresh_ref.shape[1]
    outers = gain_ref.shape[1] // PAIR // share
    own_share = place * outers + outer_here()
    index = (1 - place) * outers + outer_here()
    small = [
        (act_frames_in, act_frames_ref),
        (fresh_frames_in, fresh_frames_ref),
        (key_frames_in, key_frames_ref),
        (batch_in, batch_ref),
        (gain_in, gain_ref),
        (columns_of(own_share, batch_in, share), share_ref),
        (columns_of(index, fresh_in, share), fresh_ref),
        (columns_of(index, gain_in, share), fresh_gain_ref),
    ]
    small = [pltpu.make_async_copy(a, b, small_sems.at[n]) for n, (a, b) in enumerate(small)]
    copies, step = [], length // BLOCKS
    for b in range(BLOCKS):
        rows = pl.ds(b * step, step)
        copies.append(pltpu.make_async_copy(keys_in.at[rows], staged_ref.at[rows], sems.at[b]))
    for copy in small[:3] + copies + small[3:]:
        copy.start()
    for copy in small[:3]:
        copy.wait()

    tokens = frames_ref.shape[1]
    section = lax.axis_index("section")
    own_row = act_frames_ref[pl.ds(section, 1), :].astype(jnp.float32)
    prior_row = act_frames_ref[pl.ds(jnp.maximum(section - 1, 0), 1), :].astype(jnp.float32)
    fresh_row = fresh_frames_ref[...].astype(jnp.float32)
    next_row = jnp.where(in_first_section(), fresh_row, prior_row)
    for tick, row in enumerate((own_row, next_row)):
        frames_ref[tick] = jnp.broadcast_to(column_of(row), (tokens, HD))

    row = row_of(key_frames_ref).astype(jnp.float32)
    lines = -(-length // width)
    row = jnp.concatenate([row, jnp.zeros((1, lines * width - length), jnp.float32)], axis=1)
    line = lax.broadcasted_iota(jnp.int32, (STAT_ROWS, width), 0)
    tail = jnp.zeros((STAT_ROWS, width), jnp.float32)
    for n in range(lines):
        tail = jnp.where(line == n, row[:, n * width : (n + 1) * width], tail)
    for ref in (own_ref, given_ref):
        ref[length:] = tail.astype(jnp.bfloat16)
    halve(staged_ref, copies, own_ref, given_ref)
    for copy in small[3:]:
        copy.wait()


def load_keys(act_frames, fresh_frames, key_frames, batch, fresh, gain, keys):
    length, width = keys.shape
    tokens, model = batch.shape
    share = model * INNER // lax.axis_size("ctx")
    shape = (length + STAT_ROWS, width // PAIR)
    frames = (act_frames, fresh_frames, key_frames)
    return pl.pallas_call(
        load_keys_kernel,
        in_specs=[IN_HBM] * 7,
        out_specs=[WHOLE] * 8,
        out_shape=[
            pltpu.VMEM(shape, keys.dtype),
            pltpu.VMEM(shape, keys.dtype),
            pltpu.VMEM(batch.shape, batch.dtype),
            pltpu.VMEM(gain.shape, gain.dtype),
            pltpu.VMEM((tokens, share), batch.dtype),
            pltpu.VMEM((tokens, share), fresh.dtype),
            pltpu.VMEM((1, share), gain.dtype),
            pltpu.VMEM((2, tokens, HD), jnp.float32),
        ],
        scratch_shapes=[
            *(pltpu.VMEM(a.shape, a.dtype) for a in frames),
            pltpu.VMEM((length, width), keys.dtype),
            pltpu.SemaphoreType.DMA((BLOCKS,)),
            pltpu.SemaphoreType.DMA((8,)),
        ],
        cost_estimate=pl.CostEstimate(
            flops=0, bytes_accessed=2 * length * width, transcendentals=0
        ),
        compiler_params=pltpu.CompilerParams(vmem_limit_bytes=16 * MIB),
        name="load_keys",
    )(*in_hbm(*frames, batch, fresh, gain, keys))


def halve_values_kernel(values_ref, own_ref, given_ref):
    halve(values_ref, [], own_ref, given_ref)


def halve_values(values):
    length, width = values.shape
    half = pltpu.VMEM((length, width // PAIR), values.dtype)
    return pl.pallas_call(
        halve_values_kernel,
        in_specs=[WHOLE],
        out_specs=[WHOLE] * 2,
        out_shape=[half, half],
        cost_estimate=pl.CostEstimate(
            flops=0, bytes_accessed=2 * length * width, transcendentals=0
        ),
        compiler_params=pltpu.CompilerParams(vmem_limit_bytes=16 * MIB),
        name="halve_values",
    )(*in_vmem(values))


def first_kernel(other, gain_ref, frames_ref, batch_ref, keys_ref, values_ref, out_ref):
    length, kv_here = values_ref.shape[0], out_ref.shape[0]
    width = gain_ref.shape[1] // (PAIR * kv_here)
    place = (place_here() + other) % PAIR
    bias = bias_of(keys_ref, frames_ref[0, :, :1])
    for g in range(kv_here):
        index, block = place * kv_here + g, slice(g * HD, (g + 1) * HD)
        x, gain = columns_of(index, batch_ref, width)[...], columns_of(index, gain_ref, width)[...]
        raw = scores(queries_of(x, gain), keys_ref[:length, block], bias)
        top = top_of(raw)
        both = weigh(raw, top, values_ref[:, block])
        write_sums(out_ref.at[g], both[:, :HD], top, both[:, HD:])


def first(other, gain, frames, batch, keys, values):
    length, width = values.shape
    tokens = batch.shape[0]
    kv_here = width // HD
    queries = HEADS // PAIR * tokens
    return pl.pallas_call(
        functools.partial(first_kernel, other),
        in_specs=[WHOLE] * 5,
        out_specs=WHOLE,
        out_shape=jax.ShapeDtypeStruct((kv_here, queries // kv_here + STAT_ROWS, HD), jnp.bfloat16),
        cost_estimate=pl.CostEstimate(
            flops=2 * queries * length * 3 * HD,
            bytes_accessed=4 * length * width,
            transcendentals=queries * length,
        ),
        compiler_params=pltpu.CompilerParams(vmem_limit_bytes=16 * MIB),
        name="first",
    )(*in_vmem(gain, frames, batch, keys, values))


def finish_kernel(steps, mine_ref, got_ref, *out_refs):
    for d, out_ref in zip(steps, out_refs):
        g = outer_here() ^ d
        write_chunk(out_ref, *joined([mine_ref.at[g], got_ref.at[g]], False))


def finish(steps, mine, got):
    chunk = jax.ShapeDtypeStruct(mine.shape[1:], mine.dtype)
    return pl.pallas_call(
        functools.partial(finish_kernel, steps),
        in_specs=[WHOLE] * 2,
        out_specs=[WHOLE] * len(steps),
        out_shape=[chunk] * len(steps),
        compiler_params=pltpu.CompilerParams(vmem_limit_bytes=8 * MIB),
        name="finish",
    )(*in_vmem(mine, got))


def in_calls(call, outers, together):
    chunks, far = {}, outers - together
    for steps in [tuple(range(far, outers))[::-1]] + [(d,) for d in reversed(range(far))]:
        chunks.update(zip(steps, call(steps)))
    return [chunks[d] for d in range(outers)]


def chunk_call(kernel, name, steps, kv_here, count, length, operands):
    chunk = jax.ShapeDtypeStruct((count + STAT_ROWS, HD), jnp.bfloat16)
    return pl.pallas_call(
        functools.partial(kernel, steps, kv_here),
        in_specs=[WHOLE] * len(operands),
        out_specs=[WHOLE] * len(steps),
        out_shape=[chunk] * len(steps),
        cost_estimate=pl.CostEstimate(
            flops=2 * len(steps) * count * length * 3 * HD,
            bytes_accessed=4 * len(steps) * length * HD,
            transcendentals=len(steps) * count * length,
        ),
        compiler_params=pltpu.CompilerParams(vmem_limit_bytes=16 * MIB),
        name=name,
    )(*in_vmem(*operands))


def partials_kernel(steps, kv_here, frames_ref, *refs):
    kv_refs, refs = (refs[0:2], refs[2:4]), refs[4:]
    length = kv_refs[0][1].shape[0]
    biases = [bias_of(keys_ref, frames_ref[1, :, :1]) for keys_ref, _ in kv_refs]
    for d, queries_ref, out_ref in zip(steps, refs, refs[len(steps) :]):
        g = outer_here() ^ d
        raws = [
            scores(queries_ref[...], columns_of(g, keys_ref.at[:length], HD)[...], bias)
            for (keys_ref, _), bias in zip(kv_refs, biases)
        ]
        top = functools.reduce(jnp.maximum, [top_of(raw) for raw in raws])
        both = sum(
            weigh(raw, top, columns_of(g, values_ref, HD)[...])
            for raw, (_, values_ref) in zip(raws, kv_refs)
        )
        write_sums(out_ref, both[:, :HD], top, both[:, HD:])


def partials(steps, frames, own, got, queries):
    length, width = own[1].shape
    count = queries[0].shape[0]
    operands = (frames, *own, *got, *(queries[d] for d in steps))
    return chunk_call(
        partials_kernel, "partials", steps, width // HD, count, PAIR * length, operands
    )


def merge_kernel(*refs):
    *parts, out_ref = refs
    write_chunk(out_ref, *joined(parts, False))


def merge_first_kernel(*refs):
    *parts, share_ref, out_ref = refs
    x = head_rows(share_ref[...].astype(jnp.float32)).astype(jnp.bfloat16)
    write_chunk(out_ref, *joined(parts, False, x))


def merge(kernel, *parts):
    return pl.pallas_call(
        kernel,
        in_specs=[WHOLE] * len(parts),
        out_specs=WHOLE,
        out_shape=jax.ShapeDtypeStruct(parts[0].shape, parts[0].dtype),
        compiler_params=pltpu.CompilerParams(vmem_limit_bytes=8 * MIB),
        name="merge",
    )(*in_vmem(*parts))


def attended(one_ref, two_ref):
    one, two = one_ref[...].astype(jnp.float32), two_ref[...].astype(jnp.float32)
    here = inner_here() == 0
    parts = [jnp.where(here, one, two), jnp.where(here, two, one)]
    value, _, _ = joined([part.astype(jnp.bfloat16) for part in parts], True)
    return value


def columns_from(rows, tokens):
    pieces = [rows[at : at + tokens] for at in range(0, rows.shape[0], tokens)]
    return jnp.concatenate(pieces, axis=1)


def combine_kernel(gain_ref, fresh_ref, one_ref, two_ref, share_ref, queries_ref):
    tokens = fresh_ref.shape[0]
    handed = columns_from(attended(one_ref, two_ref), tokens).astype(jnp.bfloat16)
    fresh = fresh_ref[...].astype(jnp.float32)
    share = jnp.where(in_first_section(), fresh, handed.astype(jnp.float32))
    share = share.astype(jnp.bfloat16)
    share_ref[...] = share
    queries_ref[...] = queries_of(share, gain_ref[...])


def combine(gain, fresh, one, two):
    count = one.shape[0] - STAT_ROWS
    return pl.pallas_call(
        combine_kernel,
        in_specs=[WHOLE] * 4,
        out_specs=[WHOLE] * 2,
        out_shape=[
            jax.ShapeDtypeStruct(fresh.shape, fresh.dtype),
            jax.ShapeDtypeStruct((count, HD), jnp.bfloat16),
        ],
        compiler_params=pltpu.CompilerParams(vmem_limit_bytes=8 * MIB),
        name="combine",
    )(*in_vmem(gain, fresh, one, two))


def combine_last_kernel(share_ref, one_ref, two_ref, out_ref):
    tokens = out_ref.shape[0]
    total = head_rows(share_ref[...].astype(jnp.float32)) + attended(one_ref, two_ref)
    out_ref[...] = columns_from(total, tokens).astype(jnp.bfloat16)


def combine_last(share, one, two):
    return pl.pallas_call(
        combine_last_kernel,
        in_specs=[WHOLE] * 3,
        out_specs=WHOLE,
        out_shape=jax.ShapeDtypeStruct(share.shape, share.dtype),
        compiler_params=pltpu.CompilerParams(vmem_limit_bytes=8 * MIB),
        name="combine_last",
    )(*in_vmem(share, one, two))


def assemble_kernel(*refs):
    *pieces, out_ref = refs
    outers, width = len(pieces) // PAIR, pieces[0].shape[1]
    for n, refs in enumerate((pieces[:outers], pieces[outers:])):
        place = (place_here() + n) % PAIR
        for d, ref in enumerate(refs):
            columns_of(place * outers + (outer_here() ^ d), out_ref, width)[...] = ref[...]


def assemble(mine, others):
    tokens, width = mine[0].shape
    pieces = [*mine, *others]
    return pl.pallas_call(
        assemble_kernel,
        in_specs=[WHOLE] * len(pieces),
        out_specs=WHOLE,
        out_shape=jax.ShapeDtypeStruct((tokens, len(pieces) * width), jnp.bfloat16),
        compiler_params=pltpu.CompilerParams(vmem_limit_bytes=8 * MIB),
        name="assemble",
    )(*in_vmem(*pieces))


def body(
    activations,
    act_frames,
    fresh_batch,
    fresh_frames,
    norm_gain,
    cached_keys,
    cached_values,
    key_frames,
):
    own_keys, given_keys, batch, gain, share, fresh, fresh_gain, frames = load_keys(
        act_frames, fresh_frames[None], key_frames.reshape(-1, HD), activations[0], fresh_batch,
        norm_gain, cached_keys[0],
    )
    own_values, given_values = halve_values(cached_values[0])

    outers = lax.axis_size("ctx") // (INNER * PAIR)
    theirs = swapped(first(1, gain, frames, batch, given_keys, given_values))
    mine = first(0, gain, frames, batch, own_keys, own_values)
    chunk, *others = in_calls(lambda steps: finish(steps, mine, theirs), outers, 2)
    own, got = (own_keys, own_values), (swapped(given_keys), swapped(given_values))
    chunk = merge(merge_first_kernel, *from_outer(others, 0)[::-1], chunk, share)
    one, two = [from_section_before(chunk, step) for step in range(INNER)]
    share, queries = combine(fresh_gain, fresh, one, two)
    queries = [swapped(queries), *from_outer([queries] * len(others))]

    chunk, *others = in_calls(lambda steps: partials(steps, frames, own, got, queries), outers, 1)
    chunk = merge(merge_kernel, *from_outer(others)[::-1], swapped(chunk))
    one, two = swapped(chunk), from_inner(chunk)
    share = combine_last(swapped(share), one, two)
    theirs = [swapped(share), *from_outer([share] * len(others))]
    return assemble([share, *(swapped(piece) for piece in theirs[1:])], theirs)[None]


def solution(mesh):
    placed = (
        P("section", None, None),
        P(),
        P(),
        P(),
        P("section", None),
        P("section", "ctx", None),
        P("section", "ctx", None),
        P("ctx"),
    )
    return jax.shard_map(
        body, mesh=mesh, in_specs=placed, out_specs=P("section", None, None), check_vma=False
    )
```

profile of v0, /device:TPU:0, one launch (start us, length us, event | category | flops | bytes accessed | tf_op | source)
XLA Modules:
  0.0 53.9 jit_solution(16996306320152524322)
XLA Ops:
  0.0 1.8 %load_keys.1 = (bf16[784,512]{1,0:T(8,128)(2,1)S(1)}, bf16[784,512]{1,0:T(8,128)(2,1)S(1)}, bf16[24,8192]{1,0:T(8,128)(2,1)S(1)}, f32[1,8192]{1,0:T(1,128)S(1)},...) custom-call(s32[2,24]{1,0:T(2,128)} %act_frames_in.1, ...), custom_call_target="tpu_custom_call" | custom-call | bytes 1572864 | tf_op jit(solution)/shard_map/load_keys/pallas_call | solution.py:278
  1.8 0.5 collective-permute-start.7
  2.4 0.1 halve_values.1
  2.5 0.3 collective-permute-start.8
  2.7 1.3 %first.3 = bf16[4,208,128]{2,1,0:T(8,128)(2,1)S(1)} custom-call(f32[1,8192]{1,0:T(1,128)S(1)} %get-tuple-element.21.gain_ref, f32[2,24,128]{2,1,0:T(8,128)S(1)} %get-tuple-element.22.frames_ref, bf16[24,8192]{1,0:T(8,128)(2,1)S(1)} %get-tuple-element.23.batch_ref, bf16[784,512]{1,0:T(8,128)(2,1)S(1)} %get-tuple-element.26.keys_ref, ...), custom_call_target="tpu_custom_call" | custom-call | flops 452984832 | bytes 1572864 | tf_op jit(solution)/shard_map/first/pallas_call | solution.py:345
  4.0 0.4 collective-permute-start
  4.4 1.3 %first.2.mine_ref = bf16[4,208,128]{2,1,0:T(8,128)(2,1)S(1)} custom-call(f32[1,8192]{1,0:T(1,128)S(1)} %get-tuple-element.21.gain_ref, f32[2,24,128]{2,1,0:T(8,128)S(1)} %get-tuple-element.22.frames_ref, bf16[24,8192]{1,0:T(8,128)(2,1)S(1)} %get-tuple-element.23.batch_ref, bf16[784,512]{1,0:T(8,128)(2,1)S(1)} %get-tuple-element.24.keys_ref.refs_0_, ...), custom_call_target="tpu_custom_call" | custom-call | flops 452984832 | bytes 1572864 | tf_op jit(solution)/shard_map/first/pallas_call | solution.py:345
  5.7 0.3 finish.3
  6.0 5.0 %collective-permute-start.1 = (bf16[208,128]{1,0:T(8,128)(2,1)S(1)}, bf16[208,128]{1,0:T(8,128)(2,1)S(1)}, u32[]{:S(2)}, u32[]{:S(2)}) collective-permute-start(bf16[208,128]{1,0:T(8,128)(2,1)S(1)} %get-tuple-element.28), channel_id=1, source_target_pairs={{0,12},{1,13},{2,14},{3,15},{4,8},{5,9},{6,10},{7,11},{8,4},{9,5},... | collective-permute-start | bytes 159752 | tf_op jit(solution)/shard_map/ppermute | solution.py:63
  11.0 0.2 finish.4
  11.2 0.7 %collective-permute-start.3 = (bf16[208,128]{1,0:T(8,128)(2,1)S(1)}, bf16[208,128]{1,0:T(8,128)(2,1)S(1)}, u32[]{:S(2)}, u32[]{:S(2)}) collective-permute-start(bf16[208,128]{1,0:T(8,128)(2,1)S(1)} %finish.4), channel_id=1, source_target_pairs={{0,4},{1,5},{2,6},{3,7},{4,0},{5,1},{6,2},{7,3},{8,12},{9,13},{10,... | collective-permute-start | bytes 159752 | tf_op jit(solution)/shard_map/ppermute | solution.py:63
  11.9 0.2 finish.5.refs_3_
  12.1 1.1 %collective-permute-done.1.refs_0_ = bf16[208,128]{1,0:T(8,128)(2,1)S(1)} collective-permute-done((bf16[208,128]{1,0:T(8,128)(2,1)S(1)}, bf16[208,128]{1,0:T(8,128)(2,1)S(1)}, u32[]{:S(2)}, u32[]{:S(2)}) %collective-permute-start.1) | collective-permute-done | bytes 53280 | tf_op jit(solution)/shard_map/ppermute | solution.py:63
  13.3 2.9 %collective-permute-done.2.refs_1_ = bf16[208,128]{1,0:T(8,128)(2,1)S(1)} collective-permute-done((bf16[208,128]{1,0:T(8,128)(2,1)S(1)}, bf16[208,128]{1,0:T(8,128)(2,1)S(1)}, u32[]{:S(2)}, u32[]{:S(2)}) %collective-permute-start.2) | collective-permute-done | bytes 53280 | tf_op jit(solution)/shard_map/ppermute | solution.py:63
  16.2 0.2 collective-permute-done.3.refs_2_
  16.4 0.3 merge.2
  16.7 0.4 collective-permute-start.4
  17.1 2.3 %collective-permute-start.5 = (bf16[208,128]{1,0:T(8,128)(2,1)S(1)}, bf16[208,128]{1,0:T(8,128)(2,1)S(1)}, u32[]{:S(2)}, u32[]{:S(2)}) collective-permute-start(bf16[208,128]{1,0:T(8,128)(2,1)S(1)} %merge.2), channel_id=1, source_target_pairs={{0,19},{1,18},{2,17},{3,16},{4,23},{5,22},{6,21},{7,20},{8,27},{9,... | collective-permute-start | bytes 159752 | tf_op jit(solution)/shard_map/ppermute | solution.py:78
  19.5 1.4 %collective-permute-done.4.one_ref = bf16[208,128]{1,0:T(8,128)(2,1)S(1)} collective-permute-done((bf16[208,128]{1,0:T(8,128)(2,1)S(1)}, bf16[208,128]{1,0:T(8,128)(2,1)S(1)}, u32[]{:S(2)}, u32[]{:S(2)}) %collective-permute-start.4) | collective-permute-done | bytes 53280 | tf_op jit(solution)/shard_map/ppermute | solution.py:78
  20.8 1.6 %collective-permute-done.5.two_ref = bf16[208,128]{1,0:T(8,128)(2,1)S(1)} collective-permute-done((bf16[208,128]{1,0:T(8,128)(2,1)S(1)}, bf16[208,128]{1,0:T(8,128)(2,1)S(1)}, u32[]{:S(2)}, u32[]{:S(2)}) %collective-permute-start.5) | collective-permute-done | bytes 53280 | tf_op jit(solution)/shard_map/ppermute | solution.py:78
  22.4 0.3 combine.1
  22.7 2.2 %collective-permute-start.9 = (bf16[192,128]{1,0:T(8,128)(2,1)S(1)}, bf16[192,128]{1,0:T(8,128)(2,1)S(1)}, u32[]{:S(2)}, u32[]{:S(2)}) collective-permute-start(bf16[192,128]{1,0:T(8,128)(2,1)S(1)} %get-tuple-element.32), channel_id=1, source_target_pairs={{0,13},{1,12},{2,15},{3,14},{4,9},{5,8},{6,11},{7,10},{8,5},{9,4},... | collective-permute-start | bytes 147464 | tf_op jit(solution)/shard_map/ppermute | solution.py:63
  24.9 2.0 %collective-permute-start.13 = (bf16[192,128]{1,0:T(8,128)(2,1)S(1)}, bf16[192,128]{1,0:T(8,128)(2,1)S(1)}, u32[]{:S(2)}, u32[]{:S(2)}) collective-permute-start(bf16[192,128]{1,0:T(8,128)(2,1)S(1)} %get-tuple-element.32), channel_id=1, source_target_pairs={{0,5},{1,4},{2,7},{3,6},{4,1},{5,0},{6,3},{7,2},{8,13},{9,12},{10,... | collective-permute-start | bytes 147464 | tf_op jit(solution)/shard_map/ppermute | solution.py:63
  27.0 1.2 %collective-permute-done.9.refs_4_ = bf16[192,128]{1,0:T(8,128)(2,1)S(1)} collective-permute-done((bf16[192,128]{1,0:T(8,128)(2,1)S(1)}, bf16[192,128]{1,0:T(8,128)(2,1)S(1)}, u32[]{:S(2)}, u32[]{:S(2)}) %collective-permute-start.9) | collective-permute-done | bytes 49184 | tf_op jit(solution)/shard_map/ppermute | solution.py:63
  28.1 0.5 collective-permute-start.15
  28.7 1.0 %partials.4 = bf16[208,128]{1,0:T(8,128)(2,1)S(1)} custom-call(f32[2,24,128]{2,1,0:T(8,128)S(1)} %get-tuple-element.22.frames_ref, bf16[784,512]{1,0:T(8,128)(2,1)S(1)} %get-tuple-element.24.keys_ref.refs_0_, bf16[768,512]{1,0:T(8,128)(2,1)S(1)} %get-tuple-element.25.values_ref.refs_1_, bf16[784,512]{1,0:T(8,128)(2,1)S(1)} %collective-permute-done.7.refs_2_, ...), custom_call_target="tpu_custom_call" | custom-call | flops 226492416 | bytes 786432 | tf_op jit(solution)/shard_map/partials/pallas_call | solution.py:387
  29.6 2.2 %collective-permute-start.10 = (bf16[208,128]{1,0:T(8,128)(2,1)S(1)}, bf16[208,128]{1,0:T(8,128)(2,1)S(1)}, u32[]{:S(2)}, u32[]{:S(2)}) collective-permute-start(bf16[208,128]{1,0:T(8,128)(2,1)S(1)} %partials.4), channel_id=1, source_target_pairs={{0,13},{1,12},{2,15},{3,14},{4,9},{5,8},{6,11},{7,10},{8,5},{9,4},... | collective-permute-start | bytes 159752 | tf_op jit(solution)/shard_map/ppermute | solution.py:63
  31.8 0.9 %partials.5 = bf16[208,128]{1,0:T(8,128)(2,1)S(1)} custom-call(f32[2,24,128]{2,1,0:T(8,128)S(1)} %get-tuple-element.22.frames_ref, bf16[784,512]{1,0:T(8,128)(2,1)S(1)} %get-tuple-element.24.keys_ref.refs_0_, bf16[768,512]{1,0:T(8,128)(2,1)S(1)} %get-tuple-element.25.values_ref.refs_1_, bf16[784,512]{1,0:T(8,128)(2,1)S(1)} %collective-permute-done.7.refs_2_, ...), custom_call_target="tpu_custom_call" | custom-call | flops 226492416 | bytes 786432 | tf_op jit(solution)/shard_map/partials/pallas_call | solution.py:387
  32.9 1.0 %partials.6 = bf16[208,128]{1,0:T(8,128)(2,1)S(1)} custom-call(f32[2,24,128]{2,1,0:T(8,128)S(1)} %get-tuple-element.22.frames_ref, bf16[784,512]{1,0:T(8,128)(2,1)S(1)} %get-tuple-element.24.keys_ref.refs_0_, bf16[768,512]{1,0:T(8,128)(2,1)S(1)} %get-tuple-element.25.values_ref.refs_1_, bf16[784,512]{1,0:T(8,128)(2,1)S(1)} %collective-permute-done.7.refs_2_, ...), custom_call_target="tpu_custom_call" | custom-call | flops 226492416 | bytes 786432 | tf_op jit(solution)/shard_map/partials/pallas_call | solution.py:387
  33.8 1.6 %collective-permute-start.14 = (bf16[208,128]{1,0:T(8,128)(2,1)S(1)}, bf16[208,128]{1,0:T(8,128)(2,1)S(1)}, u32[]{:S(2)}, u32[]{:S(2)}) collective-permute-start(bf16[208,128]{1,0:T(8,128)(2,1)S(1)} %partials.6), channel_id=1, source_target_pairs={{0,5},{1,4},{2,7},{3,6},{4,1},{5,0},{6,3},{7,2},{8,13},{9,12},{10,... | collective-permute-start | bytes 159752 | tf_op jit(solution)/shard_map/ppermute | solution.py:63
  35.5 1.0 %partials.7 = bf16[208,128]{1,0:T(8,128)(2,1)S(1)} custom-call(f32[2,24,128]{2,1,0:T(8,128)S(1)} %get-tuple-element.22.frames_ref, bf16[784,512]{1,0:T(8,128)(2,1)S(1)} %get-tuple-element.24.keys_ref.refs_0_, bf16[768,512]{1,0:T(8,128)(2,1)S(1)} %get-tuple-element.25.values_ref.refs_1_, bf16[784,512]{1,0:T(8,128)(2,1)S(1)} %collective-permute-done.7.refs_2_, ...), custom_call_target="tpu_custom_call" | custom-call | flops 226492416 | bytes 786432 | tf_op jit(solution)/shard_map/partials/pallas_call | solution.py:387
  36.4 0.6 %collective-permute-start.16 = (bf16[208,128]{1,0:T(8,128)(2,1)S(1)}, bf16[208,128]{1,0:T(8,128)(2,1)S(1)}, u32[]{:S(2)}, u32[]{:S(2)}) collective-permute-start(bf16[208,128]{1,0:T(8,128)(2,1)S(1)} %partials.7), channel_id=1, source_target_pairs={{0,1},{1,0},{2,3},{3,2},{4,5},{5,4},{6,7},{7,6},{8,9},{9,8},{10,11... | collective-permute-start | bytes 159752 | tf_op jit(solution)/shard_map/ppermute | solution.py:52
  37.0 2.0 %collective-permute-done.12.refs_1_ = bf16[208,128]{1,0:T(8,128)(2,1)S(1)} collective-permute-done((bf16[208,128]{1,0:T(8,128)(2,1)S(1)}, bf16[208,128]{1,0:T(8,128)(2,1)S(1)}, u32[]{:S(2)}, u32[]{:S(2)}) %collective-permute-start.12) | collective-permute-done | bytes 53280 | tf_op jit(solution)/shard_map/ppermute | solution.py:63
  39.0 0.3 merge.3
  39.3 1.6 %collective-permute-start.18 = (bf16[208,128]{1,0:T(8,128)(2,1)S(1)}, bf16[208,128]{1,0:T(8,128)(2,1)S(1)}, u32[]{:S(2)}, u32[]{:S(2)}) collective-permute-start(bf16[208,128]{1,0:T(8,128)(2,1)S(1)} %merge.3), channel_id=1, source_target_pairs={{0,3},{1,2},{2,1},{3,0},{4,7},{5,6},{6,5},{7,4},{8,11},{9,10},{10,... | collective-permute-start | bytes 159752 | tf_op jit(solution)/shard_map/ppermute | solution.py:57
  41.0 1.1 %collective-permute-done.6.share_ref = bf16[24,1024]{1,0:T(8,128)(2,1)S(1)} collective-permute-done((bf16[24,1024]{1,0:T(8,128)(2,1)S(1)}, bf16[24,1024]{1,0:T(8,128)(2,1)S(1)}, u32[]{:S(2)}, u32[]{:S(2)}) %collective-permute-start.6) | collective-permute-done | bytes 49184 | tf_op jit(solution)/shard_map/ppermute | solution.py:52
  42.1 0.8 %collective-permute-done.18.two_ref = bf16[208,128]{1,0:T(8,128)(2,1)S(1)} collective-permute-done((bf16[208,128]{1,0:T(8,128)(2,1)S(1)}, bf16[208,128]{1,0:T(8,128)(2,1)S(1)}, u32[]{:S(2)}, u32[]{:S(2)}) %collective-permute-start.18) | collective-permute-done | bytes 53280 | tf_op jit(solution)/shard_map/ppermute | solution.py:57
  42.9 0.2 combine_last.1.refs_0_
  43.2 0.9 %collective-permute-start.19 = (bf16[24,1024]{1,0:T(8,128)(2,1)S(1)}, bf16[24,1024]{1,0:T(8,128)(2,1)S(1)}, u32[]{:S(2)}, u32[]{:S(2)}) collective-permute-start(bf16[24,1024]{1,0:T(8,128)(2,1)S(1)} %combine_last.1.refs_0_), channel_id=1, source_target_pairs={{0,5},{1,4},{2,7},{3,6},{4,1},{5,0},{6,3},{7,2},{8,13},{9,12},{10,... | collective-permute-start | bytes 147464 | tf_op jit(solution)/shard_map/ppermute | solution.py:63
  44.1 2.3 %collective-permute-start.21 = (bf16[24,1024]{1,0:T(8,128)(2,1)S(1)}, bf16[24,1024]{1,0:T(8,128)(2,1)S(1)}, u32[]{:S(2)}, u32[]{:S(2)}) collective-permute-start(bf16[24,1024]{1,0:T(8,128)(2,1)S(1)} %combine_last.1.refs_0_), channel_id=1, source_target_pairs={{0,9},{1,8},{2,11},{3,10},{4,13},{5,12},{6,15},{7,14},{8,1},{9,0},... | collective-permute-start | bytes 147464 | tf_op jit(solution)/shard_map/ppermute | solution.py:63
  46.4 0.9 %collective-permute-start.23 = (bf16[24,1024]{1,0:T(8,128)(2,1)S(1)}, bf16[24,1024]{1,0:T(8,128)(2,1)S(1)}, u32[]{:S(2)}, u32[]{:S(2)}) collective-permute-start(bf16[24,1024]{1,0:T(8,128)(2,1)S(1)} %combine_last.1.refs_0_), channel_id=1, source_target_pairs={{0,13},{1,12},{2,15},{3,14},{4,9},{5,8},{6,11},{7,10},{8,5},{9,4},... | collective-permute-start | bytes 147464 | tf_op jit(solution)/shard_map/ppermute | solution.py:63
  47.5 0.4 collective-permute-start.20
  47.9 1.9 %collective-permute-done.21.refs_6_ = bf16[24,1024]{1,0:T(8,128)(2,1)S(1)} collective-permute-done((bf16[24,1024]{1,0:T(8,128)(2,1)S(1)}, bf16[24,1024]{1,0:T(8,128)(2,1)S(1)}, u32[]{:S(2)}, u32[]{:S(2)}) %collective-permute-start.21) | collective-permute-done | bytes 49184 | tf_op jit(solution)/shard_map/ppermute | solution.py:63
  49.8 0.4 collective-permute-start.22
  50.2 1.7 %collective-permute-done.23.refs_7_ = bf16[24,1024]{1,0:T(8,128)(2,1)S(1)} collective-permute-done((bf16[24,1024]{1,0:T(8,128)(2,1)S(1)}, bf16[24,1024]{1,0:T(8,128)(2,1)S(1)}, u32[]{:S(2)}, u32[]{:S(2)}) %collective-permute-start.23) | collective-permute-done | bytes 49184 | tf_op jit(solution)/shard_map/ppermute | solution.py:63
  51.9 0.2 collective-permute-start.24
  52.1 1.0 %collective-permute-done.24.refs_3_ = bf16[24,1024]{1,0:T(8,128)(2,1)S(1)} collective-permute-done((bf16[24,1024]{1,0:T(8,128)(2,1)S(1)}, bf16[24,1024]{1,0:T(8,128)(2,1)S(1)}, u32[]{:S(2)}, u32[]{:S(2)}) %collective-permute-start.24) | collective-permute-done | bytes 49184 | tf_op jit(solution)/shard_map/ppermute | solution.py:52
  53.1 0.8 %assemble.1 = bf16[24,8192]{1,0:T(8,128)(2,1)} custom-call(bf16[24,1024]{1,0:T(8,128)(2,1)S(1)} %combine_last.1.refs_0_, bf16[24,1024]{1,0:T(8,128)(2,1)S(1)} %collective-permute-done.20.refs_1_, bf16[24,1024]{1,0:T(8,128)(2,1)S(1)} %collective-permute-done.22.refs_2_, bf16[24,1024]{1,0:T(8,128)(2,1)S(1)} %collective-permute-done.24.refs_3_, ...), custom_call_target="tpu_custom_call" | custom-call | tf_op jit(solution)/shard_map/assemble/pallas_call | solution.py:518
  (22 shorter events, 0.4 us)
Async XLA Ops:
  0.0 2.4 %copy-start = (bf16[1,768,1024]{2,1,0:T(8,128)(2,1)S(1)}, bf16[1,768,1024]{2,1,0:T(8,128)(2,1)}, u32[]{:S(2)}) copy-start(bf16[1,768,1024]{2,1,0:T(8,128)(2,1)} %param.14) | copy-start | bytes 4718596
  1.8 26.8 %collective-permute-start.7 = (bf16[784,512]{1,0:T(8,128)(2,1)S(1)}, bf16[784,512]{1,0:T(8,128)(2,1)S(1)}, u32[]{:S(2)}, u32[]{:S(2)}) collective-permute-start(bf16[784,512]{1,0:T(8,128)(2,1)S(1)} %get-tuple-element.26.keys_ref), channel_id=1, source_target_pairs={{0,1},{1,0},{2,3},{3,2},{4,5},{5,4},{6,7},{7,6},{8,9},{9,8},{10,11... | collective-permute-start | bytes 2408456 | tf_op jit(solution)/shard_map/ppermute | solution.py:52
  2.5 26.2 %collective-permute-start.8 = (bf16[768,512]{1,0:T(8,128)(2,1)S(1)}, bf16[768,512]{1,0:T(8,128)(2,1)S(1)}, u32[]{:S(2)}, u32[]{:S(2)}) collective-permute-start(bf16[768,512]{1,0:T(8,128)(2,1)S(1)} %get-tuple-element.27.values_ref), channel_id=1, source_target_pairs={{0,1},{1,0},{2,3},{3,2},{4,5},{5,4},{6,7},{7,6},{8,9},{9,8},{10,11... | collective-permute-start | bytes 2359304 | tf_op jit(solution)/shard_map/ppermute | solution.py:52
  4.0 1.7 %collective-permute-start = (bf16[4,208,128]{2,1,0:T(8,128)(2,1)S(1)}, bf16[4,208,128]{2,1,0:T(8,128)(2,1)S(1)}, u32[]{:S(2)}, u32[]{:S(2)}) collective-permute-start(bf16[4,208,128]{2,1,0:T(8,128)(2,1)S(1)} %first.3), channel_id=1, source_target_pairs={{0,1},{1,0},{2,3},{3,2},{4,5},{5,4},{6,7},{7,6},{8,9},{9,8},{10,11... | collective-permute-start | bytes 638984 | tf_op jit(solution)/shard_map/ppermute | solution.py:52
  6.0 7.3 %collective-permute-start.1 = (bf16[208,128]{1,0:T(8,128)(2,1)S(1)}, bf16[208,128]{1,0:T(8,128)(2,1)S(1)}, u32[]{:S(2)}, u32[]{:S(2)}) collective-permute-start(bf16[208,128]{1,0:T(8,128)(2,1)S(1)} %get-tuple-element.28), channel_id=1, source_target_pairs={{0,12},{1,13},{2,14},{3,15},{4,8},{5,9},{6,10},{7,11},{8,4},{9,5},... | collective-permute-start | bytes 159752 | tf_op jit(solution)/shard_map/ppermute | solution.py:63
  11.0 5.2 %collective-permute-start.2 = (bf16[208,128]{1,0:T(8,128)(2,1)S(1)}, bf16[208,128]{1,0:T(8,128)(2,1)S(1)}, u32[]{:S(2)}, u32[]{:S(2)}) collective-permute-start(bf16[208,128]{1,0:T(8,128)(2,1)S(1)} %get-tuple-element.29), channel_id=1, source_target_pairs={{0,8},{1,9},{2,10},{3,11},{4,12},{5,13},{6,14},{7,15},{8,0},{9,1},... | collective-permute-start | bytes 159752 | tf_op jit(solution)/shard_map/ppermute | solution.py:63
  11.2 5.1 %collective-permute-start.3 = (bf16[208,128]{1,0:T(8,128)(2,1)S(1)}, bf16[208,128]{1,0:T(8,128)(2,1)S(1)}, u32[]{:S(2)}, u32[]{:S(2)}) collective-permute-start(bf16[208,128]{1,0:T(8,128)(2,1)S(1)} %finish.4), channel_id=1, source_target_pairs={{0,4},{1,5},{2,6},{3,7},{4,0},{5,1},{6,2},{7,3},{8,12},{9,13},{10,... | collective-permute-start | bytes 159752 | tf_op jit(solution)/shard_map/ppermute | solution.py:63
  16.7 4.1 %collective-permute-start.4 = (bf16[208,128]{1,0:T(8,128)(2,1)S(1)}, bf16[208,128]{1,0:T(8,128)(2,1)S(1)}, u32[]{:S(2)}, u32[]{:S(2)}) collective-permute-start(bf16[208,128]{1,0:T(8,128)(2,1)S(1)} %merge.2), channel_id=1, source_target_pairs={{0,17},{1,16},{2,19},{3,18},{4,21},{5,20},{6,23},{7,22},{8,25},{9,... | collective-permute-start | bytes 159752 | tf_op jit(solution)/shard_map/ppermute | solution.py:78
  17.1 5.3 %collective-permute-start.5 = (bf16[208,128]{1,0:T(8,128)(2,1)S(1)}, bf16[208,128]{1,0:T(8,128)(2,1)S(1)}, u32[]{:S(2)}, u32[]{:S(2)}) collective-permute-start(bf16[208,128]{1,0:T(8,128)(2,1)S(1)} %merge.2), channel_id=1, source_target_pairs={{0,19},{1,18},{2,17},{3,16},{4,23},{5,22},{6,21},{7,20},{8,27},{9,... | collective-permute-start | bytes 159752 | tf_op jit(solution)/shard_map/ppermute | solution.py:78
  22.7 5.4 %collective-permute-start.9 = (bf16[192,128]{1,0:T(8,128)(2,1)S(1)}, bf16[192,128]{1,0:T(8,128)(2,1)S(1)}, u32[]{:S(2)}, u32[]{:S(2)}) collective-permute-start(bf16[192,128]{1,0:T(8,128)(2,1)S(1)} %get-tuple-element.32), channel_id=1, source_target_pairs={{0,13},{1,12},{2,15},{3,14},{4,9},{5,8},{6,11},{7,10},{8,5},{9,4},... | collective-permute-start | bytes 147464 | tf_op jit(solution)/shard_map/ppermute | solution.py:63
  24.9 6.9 %collective-permute-start.11 = (bf16[192,128]{1,0:T(8,128)(2,1)S(1)}, bf16[192,128]{1,0:T(8,128)(2,1)S(1)}, u32[]{:S(2)}, u32[]{:S(2)}) collective-permute-start(bf16[192,128]{1,0:T(8,128)(2,1)S(1)} %get-tuple-element.32), channel_id=1, source_target_pairs={{0,9},{1,8},{2,11},{3,10},{4,13},{5,12},{6,15},{7,14},{8,1},{9,0},... | collective-permute-start | bytes 147464 | tf_op jit(solution)/shard_map/ppermute | solution.py:63
  24.9 7.9 %collective-permute-start.13 = (bf16[192,128]{1,0:T(8,128)(2,1)S(1)}, bf16[192,128]{1,0:T(8,128)(2,1)S(1)}, u32[]{:S(2)}, u32[]{:S(2)}) collective-permute-start(bf16[192,128]{1,0:T(8,128)(2,1)S(1)} %get-tuple-element.32), channel_id=1, source_target_pairs={{0,5},{1,4},{2,7},{3,6},{4,1},{5,0},{6,3},{7,2},{8,13},{9,12},{10,... | collective-permute-start | bytes 147464 | tf_op jit(solution)/shard_map/ppermute | solution.py:63
  28.1 7.3 %collective-permute-start.15 = (bf16[192,128]{1,0:T(8,128)(2,1)S(1)}, bf16[192,128]{1,0:T(8,128)(2,1)S(1)}, u32[]{:S(2)}, u32[]{:S(2)}) collective-permute-start(bf16[192,128]{1,0:T(8,128)(2,1)S(1)} %get-tuple-element.32), channel_id=1, source_target_pairs={{0,1},{1,0},{2,3},{3,2},{4,5},{5,4},{6,7},{7,6},{8,9},{9,8},{10,11... | collective-permute-start | bytes 147464 | tf_op jit(solution)/shard_map/ppermute | solution.py:52
  29.6 7.4 %collective-permute-start.10 = (bf16[208,128]{1,0:T(8,128)(2,1)S(1)}, bf16[208,128]{1,0:T(8,128)(2,1)S(1)}, u32[]{:S(2)}, u32[]{:S(2)}) collective-permute-start(bf16[208,128]{1,0:T(8,128)(2,1)S(1)} %partials.4), channel_id=1, source_target_pairs={{0,13},{1,12},{2,15},{3,14},{4,9},{5,8},{6,11},{7,10},{8,5},{9,4},... | collective-permute-start | bytes 159752 | tf_op jit(solution)/shard_map/ppermute | solution.py:63
  32.8 6.2 %collective-permute-start.12 = (bf16[208,128]{1,0:T(8,128)(2,1)S(1)}, bf16[208,128]{1,0:T(8,128)(2,1)S(1)}, u32[]{:S(2)}, u32[]{:S(2)}) collective-permute-start(bf16[208,128]{1,0:T(8,128)(2,1)S(1)} %partials.5), channel_id=1, source_target_pairs={{0,9},{1,8},{2,11},{3,10},{4,13},{5,12},{6,15},{7,14},{8,1},{9,0},... | collective-permute-start | bytes 159752 | tf_op jit(solution)/shard_map/ppermute | solution.py:63
  33.8 5.1 %collective-permute-start.14 = (bf16[208,128]{1,0:T(8,128)(2,1)S(1)}, bf16[208,128]{1,0:T(8,128)(2,1)S(1)}, u32[]{:S(2)}, u32[]{:S(2)}) collective-permute-start(bf16[208,128]{1,0:T(8,128)(2,1)S(1)} %partials.6), channel_id=1, source_target_pairs={{0,5},{1,4},{2,7},{3,6},{4,1},{5,0},{6,3},{7,2},{8,13},{9,12},{10,... | collective-permute-start | bytes 159752 | tf_op jit(solution)/shard_map/ppermute | solution.py:63
  36.4 2.5 %collective-permute-start.16 = (bf16[208,128]{1,0:T(8,128)(2,1)S(1)}, bf16[208,128]{1,0:T(8,128)(2,1)S(1)}, u32[]{:S(2)}, u32[]{:S(2)}) collective-permute-start(bf16[208,128]{1,0:T(8,128)(2,1)S(1)} %partials.7), channel_id=1, source_target_pairs={{0,1},{1,0},{2,3},{3,2},{4,5},{5,4},{6,7},{7,6},{8,9},{9,8},{10,11... | collective-permute-start | bytes 159752 | tf_op jit(solution)/shard_map/ppermute | solution.py:52
  39.2 2.9 %collective-permute-start.17 = (bf16[208,128]{1,0:T(8,128)(2,1)S(1)}, bf16[208,128]{1,0:T(8,128)(2,1)S(1)}, u32[]{:S(2)}, u32[]{:S(2)}) collective-permute-start(bf16[208,128]{1,0:T(8,128)(2,1)S(1)} %merge.3), channel_id=1, source_target_pairs={{0,1},{1,0},{2,3},{3,2},{4,5},{5,4},{6,7},{7,6},{8,9},{9,8},{10,11... | collective-permute-start | bytes 159752 | tf_op jit(solution)/shard_map/ppermute | solution.py:52
  39.3 3.6 %collective-permute-start.18 = (bf16[208,128]{1,0:T(8,128)(2,1)S(1)}, bf16[208,128]{1,0:T(8,128)(2,1)S(1)}, u32[]{:S(2)}, u32[]{:S(2)}) collective-permute-start(bf16[208,128]{1,0:T(8,128)(2,1)S(1)} %merge.3), channel_id=1, source_target_pairs={{0,3},{1,2},{2,1},{3,0},{4,7},{5,6},{6,5},{7,4},{8,11},{9,10},{10,... | collective-permute-start | bytes 159752 | tf_op jit(solution)/shard_map/ppermute | solution.py:57
  40.9 1.2 %collective-permute-start.6 = (bf16[24,1024]{1,0:T(8,128)(2,1)S(1)}, bf16[24,1024]{1,0:T(8,128)(2,1)S(1)}, u32[]{:S(2)}, u32[]{:S(2)}) collective-permute-start(bf16[24,1024]{1,0:T(8,128)(2,1)S(1)} %get-tuple-element.31), channel_id=1, source_target_pairs={{0,1},{1,0},{2,3},{3,2},{4,5},{5,4},{6,7},{7,6},{8,9},{9,8},{10,11... | collective-permute-start | bytes 147464 | tf_op jit(solution)/shard_map/ppermute | solution.py:52
  43.2 4.3 %collective-permute-start.19 = (bf16[24,1024]{1,0:T(8,128)(2,1)S(1)}, bf16[24,1024]{1,0:T(8,128)(2,1)S(1)}, u32[]{:S(2)}, u32[]{:S(2)}) collective-permute-start(bf16[24,1024]{1,0:T(8,128)(2,1)S(1)} %combine_last.1.refs_0_), channel_id=1, source_target_pairs={{0,5},{1,4},{2,7},{3,6},{4,1},{5,0},{6,3},{7,2},{8,13},{9,12},{10,... | collective-permute-start | bytes 147464 | tf_op jit(solution)/shard_map/ppermute | solution.py:63
  44.1 5.7 %collective-permute-start.21 = (bf16[24,1024]{1,0:T(8,128)(2,1)S(1)}, bf16[24,1024]{1,0:T(8,128)(2,1)S(1)}, u32[]{:S(2)}, u32[]{:S(2)}) collective-permute-start(bf16[24,1024]{1,0:T(8,128)(2,1)S(1)} %combine_last.1.refs_0_), channel_id=1, source_target_pairs={{0,9},{1,8},{2,11},{3,10},{4,13},{5,12},{6,15},{7,14},{8,1},{9,0},... | collective-permute-start | bytes 147464 | tf_op jit(solution)/shard_map/ppermute | solution.py:63
  46.4 5.4 %collective-permute-start.23 = (bf16[24,1024]{1,0:T(8,128)(2,1)S(1)}, bf16[24,1024]{1,0:T(8,128)(2,1)S(1)}, u32[]{:S(2)}, u32[]{:S(2)}) collective-permute-start(bf16[24,1024]{1,0:T(8,128)(2,1)S(1)} %combine_last.1.refs_0_), channel_id=1, source_target_pairs={{0,13},{1,12},{2,15},{3,14},{4,9},{5,8},{6,11},{7,10},{8,5},{9,4},... | collective-permute-start | bytes 147464 | tf_op jit(solution)/shard_map/ppermute | solution.py:63
  47.4 4.7 %collective-permute-start.25 = (bf16[24,1024]{1,0:T(8,128)(2,1)S(1)}, bf16[24,1024]{1,0:T(8,128)(2,1)S(1)}, u32[]{:S(2)}, u32[]{:S(2)}) collective-permute-start(bf16[24,1024]{1,0:T(8,128)(2,1)S(1)} %combine_last.1.refs_0_), channel_id=1, source_target_pairs={{0,1},{1,0},{2,3},{3,2},{4,5},{5,4},{6,7},{7,6},{8,9},{9,8},{10,11... | collective-permute-start | bytes 147464 | tf_op jit(solution)/shard_map/ppermute | solution.py:52
  47.5 4.7 %collective-permute-start.20 = (bf16[24,1024]{1,0:T(8,128)(2,1)S(1)}, bf16[24,1024]{1,0:T(8,128)(2,1)S(1)}, u32[]{:S(2)}, u32[]{:S(2)}) collective-permute-start(bf16[24,1024]{1,0:T(8,128)(2,1)S(1)} %collective-permute-done.19.refs_5_), channel_id=1, source_target_pairs={{0,1},{1,0},{2,3},{3,2},{4,5},{5,4},{6,7},{7,6},{8,9},{9,8},{10,11... | collective-permute-start | bytes 147464 | tf_op jit(solution)/shard_map/ppermute | solution.py:52
  49.8 2.3 %collective-permute-start.22 = (bf16[24,1024]{1,0:T(8,128)(2,1)S(1)}, bf16[24,1024]{1,0:T(8,128)(2,1)S(1)}, u32[]{:S(2)}, u32[]{:S(2)}) collective-permute-start(bf16[24,1024]{1,0:T(8,128)(2,1)S(1)} %collective-permute-done.21.refs_6_), channel_id=1, source_target_pairs={{0,1},{1,0},{2,3},{3,2},{4,5},{5,4},{6,7},{7,6},{8,9},{9,8},{10,11... | collective-permute-start | bytes 147464 | tf_op jit(solution)/shard_map/ppermute | solution.py:52
  51.9 1.2 %collective-permute-start.24 = (bf16[24,1024]{1,0:T(8,128)(2,1)S(1)}, bf16[24,1024]{1,0:T(8,128)(2,1)S(1)}, u32[]{:S(2)}, u32[]{:S(2)}) collective-permute-start(bf16[24,1024]{1,0:T(8,128)(2,1)S(1)} %collective-permute-done.23.refs_7_), channel_id=1, source_target_pairs={{0,1},{1,0},{2,3},{3,2},{4,5},{5,4},{6,7},{7,6},{8,9},{9,8},{10,11... | collective-permute-start | bytes 147464 | tf_op jit(solution)/shard_map/ppermute | solution.py:52
where the time goes:
time: 54 us; the launch traced here: 53.9 us
  starting transfers between devices  26 us (48%)
  waiting for transfers between devices  16.9 us (31%)
  Pallas kernels  10.9 us (20%)
    ppermute x12, starting transfers between devices, from_outer(): lax.ppermute(block, 'ctx', [(i, i ^ INNER * PAIR * d ^ other_place) for i...  18.1 us
    ppermute x12, waiting for transfers between devices, from_outer(): lax.ppermute(block, 'ctx', [(i, i ^ INNER * PAIR * d ^ other_place) for i...  10.9 us
    pallas_call x4, Pallas kernels, chunk_call(): pl.pallas_call(functools.partial(kernel, steps, kv_here), in_specs=[WHOLE...  3.83 us
    ppermute x11, starting transfers between devices, swapped(): lax.ppermute(block, 'ctx', [(i, i ^ 1) for i in range(lax.axis_size('ctx'...  3.61 us
    ppermute x2, waiting for transfers between devices, from_section_before(): return lax.ppermute(block, ('section', 'ctx'), route)  2.95 us
    ppermute x2, starting transfers between devices, from_section_before(): return lax.ppermute(block, ('section', 'ctx'), route)  2.77 us
    pallas_call x2, Pallas kernels, first(): pl.pallas_call(functools.partial(first_kernel, other), in_specs=[WHOLE] *...  2.6 us
    ppermute x11, waiting for transfers between devices, swapped(): lax.ppermute(block, 'ctx', [(i, i ^ 1) for i in range(lax.axis_size('ctx'...  2.17 us
  transfers between devices with their start and end apart: 26, of which 12 were waited for; matrix products, arithmetic and copies ran while one was open for 0% of the time, Pallas kernels for 15%

commit v1 on v0

--- a/solution.py
+++ b/solution.py
@@ -486,7 +486,7 @@
     )(*in_vmem(gain, fresh, one, two))
 
 
-def combine_last_kernel(share_ref, one_ref, two_ref, out_ref):
+def combine_last_kernel(two_ref, one_ref, share_ref, out_ref):
     tokens = out_ref.shape[0]
     total = head_rows(share_ref[...].astype(jnp.float32)) + attended(one_ref, two_ref)
     out_ref[...] = columns_from(total, tokens).astype(jnp.bfloat16)
@@ -500,7 +500,7 @@
         out_shape=jax.ShapeDtypeStruct(share.shape, share.dtype),
         compiler_params=pltpu.CompilerParams(vmem_limit_bytes=8 * MIB),
         name="combine_last",
-    )(*in_vmem(share, one, two))
+    )(*in_vmem(two, one, share))
 
 
 def assemble_kernel(*refs):
@@ -508,13 +508,13 @@
     outers, width = len(pieces) // PAIR, pieces[0].shape[1]
     for n, refs in enumerate((pieces[:outers], pieces[outers:])):
         place = (place_here() + n) % PAIR
-        for d, ref in enumerate(refs):
+        for d, ref in zip(reversed(range(outers)), refs):
             columns_of(place * outers + (outer_here() ^ d), out_ref, width)[...] = ref[...]
 
 
 def assemble(mine, others):
     tokens, width = mine[0].shape
-    pieces = [*mine, *others]
+    pieces = [*mine[::-1], *others[::-1]]
     return pl.pallas_call(
         assemble_kernel,
         in_specs=[WHOLE] * len(pieces),
@@ -552,7 +552,7 @@
     queries = [swapped(queries), *from_outer([queries] * len(others))]
 
     chunk, *others = in_calls(lambda steps: partials(steps, frames, own, got, queries), outers, 1)
-    chunk = merge(merge_kernel, *from_outer(others)[::-1], swapped(chunk))
+    chunk = merge(merge_kernel, swapped(chunk), *from_outer(others))
     one, two = swapped(chunk), from_inner(chunk)
     share = combine_last(swapped(share), one, two)
     theirs = [swapped(share), *from_outer([share] * len(others))]

time: 54 us -> 53.7 us (level)
  transfers between devices with their start and end apart: 26 -> 26, of which waited for: 12 -> 13; matrix products, arithmetic and copies ran while one was open for 0% -> 0% of each run, Pallas kernels for 15% -> 15%
where the time goes in v1:
time: 53.7 us; the launch traced here: 53.6 us
  starting transfers between devices  25.8 us (48%)
  waiting for transfers between devices  16.7 us (31%)
  Pallas kernels  10.9 us (20%)
    ppermute x12, starting transfers between devices, from_outer(): lax.ppermute(block, 'ctx', [(i, i ^ INNER * PAIR * d ^ other_place) for i...  17.7 us
    ppermute x12, waiting for transfers between devices, from_outer(): lax.ppermute(block, 'ctx', [(i, i ^ INNER * PAIR * d ^ other_place) for i...  10.6 us
    ppermute x11, starting transfers between devices, swapped(): lax.ppermute(block, 'ctx', [(i, i ^ 1) for i in range(lax.axis_size('ctx'...  4.11 us
    pallas_call x4, Pallas kernels, chunk_call(): pl.pallas_call(functools.partial(kernel, steps, kv_here), in_specs=[WHOLE...  3.83 us
    ppermute x2, waiting for transfers between devices, from_section_before(): return lax.ppermute(block, ('section', 'ctx'), route)  2.95 us
    ppermute x2, starting transfers between devices, from_section_before(): return lax.ppermute(block, ('section', 'ctx'), route)  2.77 us
    pallas_call x2, Pallas kernels, first(): pl.pallas_call(functools.partial(first_kernel, other), in_specs=[WHOLE] *...  2.6 us
    ppermute x11, waiting for transfers between devices, swapped(): lax.ppermute(block, 'ctx', [(i, i ^ 1) for i in range(lax.axis_size('ctx'...  2.02 us
  transfers between devices with their start and end apart: 26, of which 13 were waited for; matrix products, arithmetic and copies ran while one was open for 0% of the time, Pallas kernels for 15%

profile of v1, /device:TPU:0, one launch (start us, length us, event | category | flops | bytes accessed | tf_op | source)
XLA Modules:
  0.0 53.6 jit_solution(11853512980209527737)
XLA Ops:
  0.0 1.8 %load_keys.1 = (bf16[784,512]{1,0:T(8,128)(2,1)S(1)}, bf16[784,512]{1,0:T(8,128)(2,1)S(1)}, bf16[24,8192]{1,0:T(8,128)(2,1)S(1)}, f32[1,8192]{1,0:T(1,128)S(1)},...) custom-call(s32[2,24]{1,0:T(2,128)} %act_frames_in.1, ...), custom_call_target="tpu_custom_call" | custom-call | bytes 1572864 | tf_op jit(solution)/shard_map/load_keys/pallas_call | solution.py:278
  1.8 0.5 collective-permute-start
  2.5 0.3 collective-permute-start.1
  2.7 1.3 %first.3 = bf16[4,208,128]{2,1,0:T(8,128)(2,1)S(1)} custom-call(f32[1,8192]{1,0:T(1,128)S(1)} %get-tuple-element.26.gain_ref, f32[2,24,128]{2,1,0:T(8,128)S(1)} %get-tuple-element.19.frames_ref, bf16[24,8192]{1,0:T(8,128)(2,1)S(1)} %get-tuple-element.27.batch_ref, bf16[784,512]{1,0:T(8,128)(2,1)S(1)} %get-tuple-element.22.keys_ref, ...), custom_call_target="tpu_custom_call" | custom-call | flops 452984832 | bytes 1572864 | tf_op jit(solution)/shard_map/first/pallas_call | solution.py:345
  4.0 0.4 collective-permute-start.2
  4.4 1.3 %first.2.mine_ref = bf16[4,208,128]{2,1,0:T(8,128)(2,1)S(1)} custom-call(f32[1,8192]{1,0:T(1,128)S(1)} %get-tuple-element.26.gain_ref, f32[2,24,128]{2,1,0:T(8,128)S(1)} %get-tuple-element.19.frames_ref, bf16[24,8192]{1,0:T(8,128)(2,1)S(1)} %get-tuple-element.27.batch_ref, bf16[784,512]{1,0:T(8,128)(2,1)S(1)} %get-tuple-element.20.keys_ref.refs_0_, ...), custom_call_target="tpu_custom_call" | custom-call | flops 452984832 | bytes 1572864 | tf_op jit(solution)/shard_map/first/pallas_call | solution.py:345
  5.7 0.3 finish.3
  6.0 5.0 %collective-permute-start.3 = (bf16[208,128]{1,0:T(8,128)(2,1)S(1)}, bf16[208,128]{1,0:T(8,128)(2,1)S(1)}, u32[]{:S(2)}, u32[]{:S(2)}) collective-permute-start(bf16[208,128]{1,0:T(8,128)(2,1)S(1)} %get-tuple-element.28), channel_id=1, source_target_pairs={{0,12},{1,13},{2,14},{3,15},{4,8},{5,9},{6,10},{7,11},{8,4},{9,5},... | collective-permute-start | bytes 159752 | tf_op jit(solution)/shard_map/ppermute | solution.py:63
  11.0 0.2 finish.4
  11.2 0.7 %collective-permute-start.5 = (bf16[208,128]{1,0:T(8,128)(2,1)S(1)}, bf16[208,128]{1,0:T(8,128)(2,1)S(1)}, u32[]{:S(2)}, u32[]{:S(2)}) collective-permute-start(bf16[208,128]{1,0:T(8,128)(2,1)S(1)} %finish.4), channel_id=1, source_target_pairs={{0,4},{1,5},{2,6},{3,7},{4,0},{5,1},{6,2},{7,3},{8,12},{9,13},{10,... | collective-permute-start | bytes 159752 | tf_op jit(solution)/shard_map/ppermute | solution.py:63
  11.9 0.2 finish.5.refs_3_
  12.1 1.1 %collective-permute-done.3.refs_0_ = bf16[208,128]{1,0:T(8,128)(2,1)S(1)} collective-permute-done((bf16[208,128]{1,0:T(8,128)(2,1)S(1)}, bf16[208,128]{1,0:T(8,128)(2,1)S(1)}, u32[]{:S(2)}, u32[]{:S(2)}) %collective-permute-start.3) | collective-permute-done | bytes 53280 | tf_op jit(solution)/shard_map/ppermute | solution.py:63
  13.3 2.9 %collective-permute-done.4.refs_1_ = bf16[208,128]{1,0:T(8,128)(2,1)S(1)} collective-permute-done((bf16[208,128]{1,0:T(8,128)(2,1)S(1)}, bf16[208,128]{1,0:T(8,128)(2,1)S(1)}, u32[]{:S(2)}, u32[]{:S(2)}) %collective-permute-start.4) | collective-permute-done | bytes 53280 | tf_op jit(solution)/shard_map/ppermute | solution.py:63
  16.2 0.2 collective-permute-done.5.refs_2_
  16.4 0.3 merge.2
  16.7 0.4 collective-permute-start.6
  17.1 2.3 %collective-permute-start.7 = (bf16[208,128]{1,0:T(8,128)(2,1)S(1)}, bf16[208,128]{1,0:T(8,128)(2,1)S(1)}, u32[]{:S(2)}, u32[]{:S(2)}) collective-permute-start(bf16[208,128]{1,0:T(8,128)(2,1)S(1)} %merge.2), channel_id=1, source_target_pairs={{0,19},{1,18},{2,17},{3,16},{4,23},{5,22},{6,21},{7,20},{8,27},{9,... | collective-permute-start | bytes 159752 | tf_op jit(solution)/shard_map/ppermute | solution.py:78
  19.5 1.4 %collective-permute-done.6.one_ref = bf16[208,128]{1,0:T(8,128)(2,1)S(1)} collective-permute-done((bf16[208,128]{1,0:T(8,128)(2,1)S(1)}, bf16[208,128]{1,0:T(8,128)(2,1)S(1)}, u32[]{:S(2)}, u32[]{:S(2)}) %collective-permute-start.6) | collective-permute-done | bytes 53280 | tf_op jit(solution)/shard_map/ppermute | solution.py:78
  20.8 1.6 %collective-permute-done.7.two_ref = bf16[208,128]{1,0:T(8,128)(2,1)S(1)} collective-permute-done((bf16[208,128]{1,0:T(8,128)(2,1)S(1)}, bf16[208,128]{1,0:T(8,128)(2,1)S(1)}, u32[]{:S(2)}, u32[]{:S(2)}) %collective-permute-start.7) | collective-permute-done | bytes 53280 | tf_op jit(solution)/shard_map/ppermute | solution.py:78
  22.4 0.3 combine.1
  22.7 2.2 %collective-permute-start.14 = (bf16[192,128]{1,0:T(8,128)(2,1)S(1)}, bf16[192,128]{1,0:T(8,128)(2,1)S(1)}, u32[]{:S(2)}, u32[]{:S(2)}) collective-permute-start(bf16[192,128]{1,0:T(8,128)(2,1)S(1)} %get-tuple-element.31), channel_id=1, source_target_pairs={{0,13},{1,12},{2,15},{3,14},{4,9},{5,8},{6,11},{7,10},{8,5},{9,4},... | collective-permute-start | bytes 147464 | tf_op jit(solution)/shard_map/ppermute | solution.py:63
  24.9 2.0 %collective-permute-start.10 = (bf16[192,128]{1,0:T(8,128)(2,1)S(1)}, bf16[192,128]{1,0:T(8,128)(2,1)S(1)}, u32[]{:S(2)}, u32[]{:S(2)}) collective-permute-start(bf16[192,128]{1,0:T(8,128)(2,1)S(1)} %get-tuple-element.31), channel_id=1, source_target_pairs={{0,5},{1,4},{2,7},{3,6},{4,1},{5,0},{6,3},{7,2},{8,13},{9,12},{10,... | collective-permute-start | bytes 147464 | tf_op jit(solution)/shard_map/ppermute | solution.py:63
  27.0 1.2 %collective-permute-done.14.refs_4_ = bf16[192,128]{1,0:T(8,128)(2,1)S(1)} collective-permute-done((bf16[192,128]{1,0:T(8,128)(2,1)S(1)}, bf16[192,128]{1,0:T(8,128)(2,1)S(1)}, u32[]{:S(2)}, u32[]{:S(2)}) %collective-permute-start.14) | collective-permute-done | bytes 49184 | tf_op jit(solution)/shard_map/ppermute | solution.py:63
  28.1 0.5 %collective-permute-start.8 = (bf16[192,128]{1,0:T(8,128)(2,1)S(1)}, bf16[192,128]{1,0:T(8,128)(2,1)S(1)}, u32[]{:S(2)}, u32[]{:S(2)}) collective-permute-start(bf16[192,128]{1,0:T(8,128)(2,1)S(1)} %get-tuple-element.31), channel_id=1, source_target_pairs={{0,1},{1,0},{2,3},{3,2},{4,5},{5,4},{6,7},{7,6},{8,9},{9,8},{10,11... | collective-permute-start | bytes 147464 | tf_op jit(solution)/shard_map/ppermute | solution.py:52
  28.7 1.0 %partials.7 = bf16[208,128]{1,0:T(8,128)(2,1)S(1)} custom-call(f32[2,24,128]{2,1,0:T(8,128)S(1)} %get-tuple-element.19.frames_ref, bf16[784,512]{1,0:T(8,128)(2,1)S(1)} %get-tuple-element.20.keys_ref.refs_0_, bf16[768,512]{1,0:T(8,128)(2,1)S(1)} %get-tuple-element.21.values_ref.refs_1_, bf16[784,512]{1,0:T(8,128)(2,1)S(1)} %collective-permute-done.refs_2_, ...), custom_call_target="tpu_custom_call" | custom-call | flops 226492416 | bytes 786432 | tf_op jit(solution)/shard_map/partials/pallas_call | solution.py:387
  29.6 2.2 %collective-permute-start.15 = (bf16[208,128]{1,0:T(8,128)(2,1)S(1)}, bf16[208,128]{1,0:T(8,128)(2,1)S(1)}, u32[]{:S(2)}, u32[]{:S(2)}) collective-permute-start(bf16[208,128]{1,0:T(8,128)(2,1)S(1)} %partials.7), channel_id=1, source_target_pairs={{0,13},{1,12},{2,15},{3,14},{4,9},{5,8},{6,11},{7,10},{8,5},{9,4},... | collective-permute-start | bytes 159752 | tf_op jit(solution)/shard_map/ppermute | solution.py:63
  31.8 0.9 %partials.6 = bf16[208,128]{1,0:T(8,128)(2,1)S(1)} custom-call(f32[2,24,128]{2,1,0:T(8,128)S(1)} %get-tuple-element.19.frames_ref, bf16[784,512]{1,0:T(8,128)(2,1)S(1)} %get-tuple-element.20.keys_ref.refs_0_, bf16[768,512]{1,0:T(8,128)(2,1)S(1)} %get-tuple-element.21.values_ref.refs_1_, bf16[784,512]{1,0:T(8,128)(2,1)S(1)} %collective-permute-done.refs_2_, ...), custom_call_target="tpu_custom_call" | custom-call | flops 226492416 | bytes 786432 | tf_op jit(solution)/shard_map/partials/pallas_call | solution.py:387
  32.9 1.0 %partials.5 = bf16[208,128]{1,0:T(8,128)(2,1)S(1)} custom-call(f32[2,24,128]{2,1,0:T(8,128)S(1)} %get-tuple-element.19.frames_ref, bf16[784,512]{1,0:T(8,128)(2,1)S(1)} %get-tuple-element.20.keys_ref.refs_0_, bf16[768,512]{1,0:T(8,128)(2,1)S(1)} %get-tuple-element.21.values_ref.refs_1_, bf16[784,512]{1,0:T(8,128)(2,1)S(1)} %collective-permute-done.refs_2_, ...), custom_call_target="tpu_custom_call" | custom-call | flops 226492416 | bytes 786432 | tf_op jit(solution)/shard_map/partials/pallas_call | solution.py:387
  33.8 1.6 %collective-permute-start.11 = (bf16[208,128]{1,0:T(8,128)(2,1)S(1)}, bf16[208,128]{1,0:T(8,128)(2,1)S(1)}, u32[]{:S(2)}, u32[]{:S(2)}) collective-permute-start(bf16[208,128]{1,0:T(8,128)(2,1)S(1)} %partials.5), channel_id=1, source_target_pairs={{0,5},{1,4},{2,7},{3,6},{4,1},{5,0},{6,3},{7,2},{8,13},{9,12},{10,... | collective-permute-start | bytes 159752 | tf_op jit(solution)/shard_map/ppermute | solution.py:63
  35.5 1.0 %partials.4 = bf16[208,128]{1,0:T(8,128)(2,1)S(1)} custom-call(f32[2,24,128]{2,1,0:T(8,128)S(1)} %get-tuple-element.19.frames_ref, bf16[784,512]{1,0:T(8,128)(2,1)S(1)} %get-tuple-element.20.keys_ref.refs_0_, bf16[768,512]{1,0:T(8,128)(2,1)S(1)} %get-tuple-element.21.values_ref.refs_1_, bf16[784,512]{1,0:T(8,128)(2,1)S(1)} %collective-permute-done.refs_2_, ...), custom_call_target="tpu_custom_call" | custom-call | flops 226492416 | bytes 786432 | tf_op jit(solution)/shard_map/partials/pallas_call | solution.py:387
  36.4 0.6 %collective-permute-start.9 = (bf16[208,128]{1,0:T(8,128)(2,1)S(1)}, bf16[208,128]{1,0:T(8,128)(2,1)S(1)}, u32[]{:S(2)}, u32[]{:S(2)}) collective-permute-start(bf16[208,128]{1,0:T(8,128)(2,1)S(1)} %partials.4), channel_id=1, source_target_pairs={{0,1},{1,0},{2,3},{3,2},{4,5},{5,4},{6,7},{7,6},{8,9},{9,8},{10,11... | collective-permute-start | bytes 159752 | tf_op jit(solution)/shard_map/ppermute | solution.py:52
  37.0 2.0 %collective-permute-done.13.refs_2_ = bf16[208,128]{1,0:T(8,128)(2,1)S(1)} collective-permute-done((bf16[208,128]{1,0:T(8,128)(2,1)S(1)}, bf16[208,128]{1,0:T(8,128)(2,1)S(1)}, u32[]{:S(2)}, u32[]{:S(2)}) %collective-permute-start.13) | collective-permute-done | bytes 53280 | tf_op jit(solution)/shard_map/ppermute | solution.py:63
  39.0 0.3 merge.3
  39.2 1.2 %collective-permute-start.16 = (bf16[208,128]{1,0:T(8,128)(2,1)S(1)}, bf16[208,128]{1,0:T(8,128)(2,1)S(1)}, u32[]{:S(2)}, u32[]{:S(2)}) collective-permute-start(bf16[208,128]{1,0:T(8,128)(2,1)S(1)} %merge.3), channel_id=1, source_target_pairs={{0,3},{1,2},{2,1},{3,0},{4,7},{5,6},{6,5},{7,4},{8,11},{9,10},{10,... | collective-permute-start | bytes 159752 | tf_op jit(solution)/shard_map/ppermute | solution.py:57
  40.5 0.4 collective-permute-start.17
  41.0 1.1 %collective-permute-done.18.share_ref = bf16[24,1024]{1,0:T(8,128)(2,1)S(1)} collective-permute-done((bf16[24,1024]{1,0:T(8,128)(2,1)S(1)}, bf16[24,1024]{1,0:T(8,128)(2,1)S(1)}, u32[]{:S(2)}, u32[]{:S(2)}) %collective-permute-start.18) | collective-permute-done | bytes 49184 | tf_op jit(solution)/shard_map/ppermute | solution.py:52
  42.1 1.1 %collective-permute-done.16.two_ref = bf16[208,128]{1,0:T(8,128)(2,1)S(1)} collective-permute-done((bf16[208,128]{1,0:T(8,128)(2,1)S(1)}, bf16[208,128]{1,0:T(8,128)(2,1)S(1)}, u32[]{:S(2)}, u32[]{:S(2)}) %collective-permute-start.16) | collective-permute-done | bytes 53280 | tf_op jit(solution)/shard_map/ppermute | solution.py:57
  43.2 0.2 combine_last.1.refs_3_
  43.4 2.5 %collective-permute-start.19 = (bf16[24,1024]{1,0:T(8,128)(2,1)S(1)}, bf16[24,1024]{1,0:T(8,128)(2,1)S(1)}, u32[]{:S(2)}, u32[]{:S(2)}) collective-permute-start(bf16[24,1024]{1,0:T(8,128)(2,1)S(1)} %combine_last.1.refs_3_), channel_id=1, source_target_pairs={{0,13},{1,12},{2,15},{3,14},{4,9},{5,8},{6,11},{7,10},{8,5},{9,4},... | collective-permute-start | bytes 147464 | tf_op jit(solution)/shard_map/ppermute | solution.py:63
  45.9 1.4 %collective-permute-start.23 = (bf16[24,1024]{1,0:T(8,128)(2,1)S(1)}, bf16[24,1024]{1,0:T(8,128)(2,1)S(1)}, u32[]{:S(2)}, u32[]{:S(2)}) collective-permute-start(bf16[24,1024]{1,0:T(8,128)(2,1)S(1)} %combine_last.1.refs_3_), channel_id=1, source_target_pairs={{0,5},{1,4},{2,7},{3,6},{4,1},{5,0},{6,3},{7,2},{8,13},{9,12},{10,... | collective-permute-start | bytes 147464 | tf_op jit(solution)/shard_map/ppermute | solution.py:63
  47.3 0.4 collective-permute-start.25
  47.8 1.3 %collective-permute-done.19.refs_4_ = bf16[24,1024]{1,0:T(8,128)(2,1)S(1)} collective-permute-done((bf16[24,1024]{1,0:T(8,128)(2,1)S(1)}, bf16[24,1024]{1,0:T(8,128)(2,1)S(1)}, u32[]{:S(2)}, u32[]{:S(2)}) %collective-permute-start.19) | collective-permute-done | bytes 49184 | tf_op jit(solution)/shard_map/ppermute | solution.py:63
  49.1 0.4 collective-permute-start.20
  49.5 1.9 %collective-permute-done.21.refs_5_ = bf16[24,1024]{1,0:T(8,128)(2,1)S(1)} collective-permute-done((bf16[24,1024]{1,0:T(8,128)(2,1)S(1)}, bf16[24,1024]{1,0:T(8,128)(2,1)S(1)}, u32[]{:S(2)}, u32[]{:S(2)}) %collective-permute-start.21) | collective-permute-done | bytes 49184 | tf_op jit(solution)/shard_map/ppermute | solution.py:63
  51.5 0.4 collective-permute-start.24
  51.9 0.7 %collective-permute-done.22.refs_1_ = bf16[24,1024]{1,0:T(8,128)(2,1)S(1)} collective-permute-done((bf16[24,1024]{1,0:T(8,128)(2,1)S(1)}, bf16[24,1024]{1,0:T(8,128)(2,1)S(1)}, u32[]{:S(2)}, u32[]{:S(2)}) %collective-permute-start.22) | collective-permute-done | bytes 49184 | tf_op jit(solution)/shard_map/ppermute | solution.py:52
  52.6 0.2 collective-permute-done.24.refs_2_
  52.8 0.8 %assemble.1 = bf16[24,8192]{1,0:T(8,128)(2,1)} custom-call(bf16[24,1024]{1,0:T(8,128)(2,1)S(1)} %collective-permute-done.20.refs_0_, bf16[24,1024]{1,0:T(8,128)(2,1)S(1)} %collective-permute-done.22.refs_1_, bf16[24,1024]{1,0:T(8,128)(2,1)S(1)} %collective-permute-done.24.refs_2_, bf16[24,1024]{1,0:T(8,128)(2,1)S(1)} %combine_last.1.refs_3_, ...), custom_call_target="tpu_custom_call" | custom-call | tf_op jit(solution)/shard_map/assemble/pallas_call | solution.py:518
  (22 shorter events, 0.5 us)
Async XLA Ops:
  0.0 2.4 %copy-start = (bf16[1,768,1024]{2,1,0:T(8,128)(2,1)S(1)}, bf16[1,768,1024]{2,1,0:T(8,128)(2,1)}, u32[]{:S(2)}) copy-start(bf16[1,768,1024]{2,1,0:T(8,128)(2,1)} %param.14) | copy-start | bytes 4718596
  1.8 26.8 %collective-permute-start = (bf16[784,512]{1,0:T(8,128)(2,1)S(1)}, bf16[784,512]{1,0:T(8,128)(2,1)S(1)}, u32[]{:S(2)}, u32[]{:S(2)}) collective-permute-start(bf16[784,512]{1,0:T(8,128)(2,1)S(1)} %get-tuple-element.22.keys_ref), channel_id=1, source_target_pairs={{0,1},{1,0},{2,3},{3,2},{4,5},{5,4},{6,7},{7,6},{8,9},{9,8},{10,11... | collective-permute-start | bytes 2408456 | tf_op jit(solution)/shard_map/ppermute | solution.py:52
  2.5 26.2 %collective-permute-start.1 = (bf16[768,512]{1,0:T(8,128)(2,1)S(1)}, bf16[768,512]{1,0:T(8,128)(2,1)S(1)}, u32[]{:S(2)}, u32[]{:S(2)}) collective-permute-start(bf16[768,512]{1,0:T(8,128)(2,1)S(1)} %get-tuple-element.23.values_ref), channel_id=1, source_target_pairs={{0,1},{1,0},{2,3},{3,2},{4,5},{5,4},{6,7},{7,6},{8,9},{9,8},{10,11... | collective-permute-start | bytes 2359304 | tf_op jit(solution)/shard_map/ppermute | solution.py:52
  4.0 1.7 %collective-permute-start.2 = (bf16[4,208,128]{2,1,0:T(8,128)(2,1)S(1)}, bf16[4,208,128]{2,1,0:T(8,128)(2,1)S(1)}, u32[]{:S(2)}, u32[]{:S(2)}) collective-permute-start(bf16[4,208,128]{2,1,0:T(8,128)(2,1)S(1)} %first.3), channel_id=1, source_target_pairs={{0,1},{1,0},{2,3},{3,2},{4,5},{5,4},{6,7},{7,6},{8,9},{9,8},{10,11... | collective-permute-start | bytes 638984 | tf_op jit(solution)/shard_map/ppermute | solution.py:52
  6.0 7.3 %collective-permute-start.3 = (bf16[208,128]{1,0:T(8,128)(2,1)S(1)}, bf16[208,128]{1,0:T(8,128)(2,1)S(1)}, u32[]{:S(2)}, u32[]{:S(2)}) collective-permute-start(bf16[208,128]{1,0:T(8,128)(2,1)S(1)} %get-tuple-element.28), channel_id=1, source_target_pairs={{0,12},{1,13},{2,14},{3,15},{4,8},{5,9},{6,10},{7,11},{8,4},{9,5},... | collective-permute-start | bytes 159752 | tf_op jit(solution)/shard_map/ppermute | solution.py:63
  11.0 5.2 %collective-permute-start.4 = (bf16[208,128]{1,0:T(8,128)(2,1)S(1)}, bf16[208,128]{1,0:T(8,128)(2,1)S(1)}, u32[]{:S(2)}, u32[]{:S(2)}) collective-permute-start(bf16[208,128]{1,0:T(8,128)(2,1)S(1)} %get-tuple-element.29), channel_id=1, source_target_pairs={{0,8},{1,9},{2,10},{3,11},{4,12},{5,13},{6,14},{7,15},{8,0},{9,1},... | collective-permute-start | bytes 159752 | tf_op jit(solution)/shard_map/ppermute | solution.py:63
  11.2 5.1 %collective-permute-start.5 = (bf16[208,128]{1,0:T(8,128)(2,1)S(1)}, bf16[208,128]{1,0:T(8,128)(2,1)S(1)}, u32[]{:S(2)}, u32[]{:S(2)}) collective-permute-start(bf16[208,128]{1,0:T(8,128)(2,1)S(1)} %finish.4), channel_id=1, source_target_pairs={{0,4},{1,5},{2,6},{3,7},{4,0},{5,1},{6,2},{7,3},{8,12},{9,13},{10,... | collective-permute-start | bytes 159752 | tf_op jit(solution)/shard_map/ppermute | solution.py:63
  16.7 4.1 %collective-permute-start.6 = (bf16[208,128]{1,0:T(8,128)(2,1)S(1)}, bf16[208,128]{1,0:T(8,128)(2,1)S(1)}, u32[]{:S(2)}, u32[]{:S(2)}) collective-permute-start(bf16[208,128]{1,0:T(8,128)(2,1)S(1)} %merge.2), channel_id=1, source_target_pairs={{0,17},{1,16},{2,19},{3,18},{4,21},{5,20},{6,23},{7,22},{8,25},{9,... | collective-permute-start | bytes 159752 | tf_op jit(solution)/shard_map/ppermute | solution.py:78
  17.1 5.3 %collective-permute-start.7 = (bf16[208,128]{1,0:T(8,128)(2,1)S(1)}, bf16[208,128]{1,0:T(8,128)(2,1)S(1)}, u32[]{:S(2)}, u32[]{:S(2)}) collective-permute-start(bf16[208,128]{1,0:T(8,128)(2,1)S(1)} %merge.2), channel_id=1, source_target_pairs={{0,19},{1,18},{2,17},{3,16},{4,23},{5,22},{6,21},{7,20},{8,27},{9,... | collective-permute-start | bytes 159752 | tf_op jit(solution)/shard_map/ppermute | solution.py:78
  22.7 5.4 %collective-permute-start.14 = (bf16[192,128]{1,0:T(8,128)(2,1)S(1)}, bf16[192,128]{1,0:T(8,128)(2,1)S(1)}, u32[]{:S(2)}, u32[]{:S(2)}) collective-permute-start(bf16[192,128]{1,0:T(8,128)(2,1)S(1)} %get-tuple-element.31), channel_id=1, source_target_pairs={{0,13},{1,12},{2,15},{3,14},{4,9},{5,8},{6,11},{7,10},{8,5},{9,4},... | collective-permute-start | bytes 147464 | tf_op jit(solution)/shard_map/ppermute | solution.py:63
  24.9 6.9 %collective-permute-start.12 = (bf16[192,128]{1,0:T(8,128)(2,1)S(1)}, bf16[192,128]{1,0:T(8,128)(2,1)S(1)}, u32[]{:S(2)}, u32[]{:S(2)}) collective-permute-start(bf16[192,128]{1,0:T(8,128)(2,1)S(1)} %get-tuple-element.31), channel_id=1, source_target_pairs={{0,9},{1,8},{2,11},{3,10},{4,13},{5,12},{6,15},{7,14},{8,1},{9,0},... | collective-permute-start | bytes 147464 | tf_op jit(solution)/shard_map/ppermute | solution.py:63
  24.9 7.9 %collective-permute-start.10 = (bf16[192,128]{1,0:T(8,128)(2,1)S(1)}, bf16[192,128]{1,0:T(8,128)(2,1)S(1)}, u32[]{:S(2)}, u32[]{:S(2)}) collective-permute-start(bf16[192,128]{1,0:T(8,128)(2,1)S(1)} %get-tuple-element.31), channel_id=1, source_target_pairs={{0,5},{1,4},{2,7},{3,6},{4,1},{5,0},{6,3},{7,2},{8,13},{9,12},{10,... | collective-permute-start | bytes 147464 | tf_op jit(solution)/shard_map/ppermute | solution.py:63
  28.1 7.3 %collective-permute-start.8 = (bf16[192,128]{1,0:T(8,128)(2,1)S(1)}, bf16[192,128]{1,0:T(8,128)(2,1)S(1)}, u32[]{:S(2)}, u32[]{:S(2)}) collective-permute-start(bf16[192,128]{1,0:T(8,128)(2,1)S(1)} %get-tuple-element.31), channel_id=1, source_target_pairs={{0,1},{1,0},{2,3},{3,2},{4,5},{5,4},{6,7},{7,6},{8,9},{9,8},{10,11... | collective-permute-start | bytes 147464 | tf_op jit(solution)/shard_map/ppermute | solution.py:52
  29.6 7.4 %collective-permute-start.15 = (bf16[208,128]{1,0:T(8,128)(2,1)S(1)}, bf16[208,128]{1,0:T(8,128)(2,1)S(1)}, u32[]{:S(2)}, u32[]{:S(2)}) collective-permute-start(bf16[208,128]{1,0:T(8,128)(2,1)S(1)} %partials.7), channel_id=1, source_target_pairs={{0,13},{1,12},{2,15},{3,14},{4,9},{5,8},{6,11},{7,10},{8,5},{9,4},... | collective-permute-start | bytes 159752 | tf_op jit(solution)/shard_map/ppermute | solution.py:63
  32.8 6.2 %collective-permute-start.13 = (bf16[208,128]{1,0:T(8,128)(2,1)S(1)}, bf16[208,128]{1,0:T(8,128)(2,1)S(1)}, u32[]{:S(2)}, u32[]{:S(2)}) collective-permute-start(bf16[208,128]{1,0:T(8,128)(2,1)S(1)} %partials.6), channel_id=1, source_target_pairs={{0,9},{1,8},{2,11},{3,10},{4,13},{5,12},{6,15},{7,14},{8,1},{9,0},... | collective-permute-start | bytes 159752 | tf_op jit(solution)/shard_map/ppermute | solution.py:63
  33.8 5.1 %collective-permute-start.11 = (bf16[208,128]{1,0:T(8,128)(2,1)S(1)}, bf16[208,128]{1,0:T(8,128)(2,1)S(1)}, u32[]{:S(2)}, u32[]{:S(2)}) collective-permute-start(bf16[208,128]{1,0:T(8,128)(2,1)S(1)} %partials.5), channel_id=1, source_target_pairs={{0,5},{1,4},{2,7},{3,6},{4,1},{5,0},{6,3},{7,2},{8,13},{9,12},{10,... | collective-permute-start | bytes 159752 | tf_op jit(solution)/shard_map/ppermute | solution.py:63
  36.4 2.5 %collective-permute-start.9 = (bf16[208,128]{1,0:T(8,128)(2,1)S(1)}, bf16[208,128]{1,0:T(8,128)(2,1)S(1)}, u32[]{:S(2)}, u32[]{:S(2)}) collective-permute-start(bf16[208,128]{1,0:T(8,128)(2,1)S(1)} %partials.4), channel_id=1, source_target_pairs={{0,1},{1,0},{2,3},{3,2},{4,5},{5,4},{6,7},{7,6},{8,9},{9,8},{10,11... | collective-permute-start | bytes 159752 | tf_op jit(solution)/shard_map/ppermute | solution.py:52
  39.2 4.0 %collective-permute-start.16 = (bf16[208,128]{1,0:T(8,128)(2,1)S(1)}, bf16[208,128]{1,0:T(8,128)(2,1)S(1)}, u32[]{:S(2)}, u32[]{:S(2)}) collective-permute-start(bf16[208,128]{1,0:T(8,128)(2,1)S(1)} %merge.3), channel_id=1, source_target_pairs={{0,3},{1,2},{2,1},{3,0},{4,7},{5,6},{6,5},{7,4},{8,11},{9,10},{10,... | collective-permute-start | bytes 159752 | tf_op jit(solution)/shard_map/ppermute | solution.py:57
  40.5 2.8 %collective-permute-start.17 = (bf16[208,128]{1,0:T(8,128)(2,1)S(1)}, bf16[208,128]{1,0:T(8,128)(2,1)S(1)}, u32[]{:S(2)}, u32[]{:S(2)}) collective-permute-start(bf16[208,128]{1,0:T(8,128)(2,1)S(1)} %merge.3), channel_id=1, source_target_pairs={{0,1},{1,0},{2,3},{3,2},{4,5},{5,4},{6,7},{7,6},{8,9},{9,8},{10,11... | collective-permute-start | bytes 159752 | tf_op jit(solution)/shard_map/ppermute | solution.py:52
  40.9 1.2 %collective-permute-start.18 = (bf16[24,1024]{1,0:T(8,128)(2,1)S(1)}, bf16[24,1024]{1,0:T(8,128)(2,1)S(1)}, u32[]{:S(2)}, u32[]{:S(2)}) collective-permute-start(bf16[24,1024]{1,0:T(8,128)(2,1)S(1)} %get-tuple-element.32), channel_id=1, source_target_pairs={{0,1},{1,0},{2,3},{3,2},{4,5},{5,4},{6,7},{7,6},{8,9},{9,8},{10,11... | collective-permute-start | bytes 147464 | tf_op jit(solution)/shard_map/ppermute | solution.py:52
  43.4 5.6 %collective-permute-start.19 = (bf16[24,1024]{1,0:T(8,128)(2,1)S(1)}, bf16[24,1024]{1,0:T(8,128)(2,1)S(1)}, u32[]{:S(2)}, u32[]{:S(2)}) collective-permute-start(bf16[24,1024]{1,0:T(8,128)(2,1)S(1)} %combine_last.1.refs_3_), channel_id=1, source_target_pairs={{0,13},{1,12},{2,15},{3,14},{4,9},{5,8},{6,11},{7,10},{8,5},{9,4},... | collective-permute-start | bytes 147464 | tf_op jit(solution)/shard_map/ppermute | solution.py:63
  45.9 5.5 %collective-permute-start.21 = (bf16[24,1024]{1,0:T(8,128)(2,1)S(1)}, bf16[24,1024]{1,0:T(8,128)(2,1)S(1)}, u32[]{:S(2)}, u32[]{:S(2)}) collective-permute-start(bf16[24,1024]{1,0:T(8,128)(2,1)S(1)} %combine_last.1.refs_3_), channel_id=1, source_target_pairs={{0,9},{1,8},{2,11},{3,10},{4,13},{5,12},{6,15},{7,14},{8,1},{9,0},... | collective-permute-start | bytes 147464 | tf_op jit(solution)/shard_map/ppermute | solution.py:63
  45.9 5.6 %collective-permute-start.23 = (bf16[24,1024]{1,0:T(8,128)(2,1)S(1)}, bf16[24,1024]{1,0:T(8,128)(2,1)S(1)}, u32[]{:S(2)}, u32[]{:S(2)}) collective-permute-start(bf16[24,1024]{1,0:T(8,128)(2,1)S(1)} %combine_last.1.refs_3_), channel_id=1, source_target_pairs={{0,5},{1,4},{2,7},{3,6},{4,1},{5,0},{6,3},{7,2},{8,13},{9,12},{10,... | collective-permute-start | bytes 147464 | tf_op jit(solution)/shard_map/ppermute | solution.py:63
  47.3 4.6 %collective-permute-start.25 = (bf16[24,1024]{1,0:T(8,128)(2,1)S(1)}, bf16[24,1024]{1,0:T(8,128)(2,1)S(1)}, u32[]{:S(2)}, u32[]{:S(2)}) collective-permute-start(bf16[24,1024]{1,0:T(8,128)(2,1)S(1)} %combine_last.1.refs_3_), channel_id=1, source_target_pairs={{0,1},{1,0},{2,3},{3,2},{4,5},{5,4},{6,7},{7,6},{8,9},{9,8},{10,11... | collective-permute-start | bytes 147464 | tf_op jit(solution)/shard_map/ppermute | solution.py:52
  49.1 2.9 %collective-permute-start.20 = (bf16[24,1024]{1,0:T(8,128)(2,1)S(1)}, bf16[24,1024]{1,0:T(8,128)(2,1)S(1)}, u32[]{:S(2)}, u32[]{:S(2)}) collective-permute-start(bf16[24,1024]{1,0:T(8,128)(2,1)S(1)} %collective-permute-done.19.refs_4_), channel_id=1, source_target_pairs={{0,1},{1,0},{2,3},{3,2},{4,5},{5,4},{6,7},{7,6},{8,9},{9,8},{10,11... | collective-permute-start | bytes 147464 | tf_op jit(solution)/shard_map/ppermute | solution.py:52
  51.4 1.2 %collective-permute-start.22 = (bf16[24,1024]{1,0:T(8,128)(2,1)S(1)}, bf16[24,1024]{1,0:T(8,128)(2,1)S(1)}, u32[]{:S(2)}, u32[]{:S(2)}) collective-permute-start(bf16[24,1024]{1,0:T(8,128)(2,1)S(1)} %collective-permute-done.21.refs_5_), channel_id=1, source_target_pairs={{0,1},{1,0},{2,3},{3,2},{4,5},{5,4},{6,7},{7,6},{8,9},{9,8},{10,11... | collective-permute-start | bytes 147464 | tf_op jit(solution)/shard_map/ppermute | solution.py:52
  51.5 1.3 %collective-permute-start.24 = (bf16[24,1024]{1,0:T(8,128)(2,1)S(1)}, bf16[24,1024]{1,0:T(8,128)(2,1)S(1)}, u32[]{:S(2)}, u32[]{:S(2)}) collective-permute-start(bf16[24,1024]{1,0:T(8,128)(2,1)S(1)} %collective-permute-done.23.refs_6_), channel_id=1, source_target_pairs={{0,1},{1,0},{2,3},{3,2},{4,5},{5,4},{6,7},{7,6},{8,9},{9,8},{10,11... | collective-permute-start | bytes 147464 | tf_op jit(solution)/shard_map/ppermute | solution.py:52

commit v2 on v1

--- a/solution.py
+++ b/solution.py
@@ -544,7 +544,7 @@
     outers = lax.axis_size("ctx") // (INNER * PAIR)
     theirs = swapped(first(1, gain, frames, batch, given_keys, given_values))
     mine = first(0, gain, frames, batch, own_keys, own_values)
-    chunk, *others = in_calls(lambda steps: finish(steps, mine, theirs), outers, 2)
+    chunk, *others = in_calls(lambda steps: finish(steps, mine, theirs), outers, outers - 1)
     own, got = (own_keys, own_values), (swapped(given_keys), swapped(given_values))
     chunk = merge(merge_first_kernel, *from_outer(others, 0)[::-1], chunk, share)
     one, two = [from_section_before(chunk, step) for step in range(INNER)]

time: 53.7 us -> 53.6 us (level)
  transfers between devices with their start and end apart: 26 -> 26, of which waited for: 13 -> 13; matrix products, arithmetic and copies ran while one was open for 0% -> 0% of each run, Pallas kernels for 15% -> 14%
where the time goes in v2:
time: 53.6 us; the launch traced here: 53.5 us
  starting transfers between devices  25.5 us (48%)
  waiting for transfers between devices  17.1 us (32%)
  Pallas kernels  10.8 us (20%)
    ppermute x12, starting transfers between devices, from_outer(): lax.ppermute(block, 'ctx', [(i, i ^ INNER * PAIR * d ^ other_place) for i...  17.7 us
    ppermute x12, waiting for transfers between devices, from_outer(): lax.ppermute(block, 'ctx', [(i, i ^ INNER * PAIR * d ^ other_place) for i...  10.9 us
    ppermute x11, starting transfers between devices, swapped(): lax.ppermute(block, 'ctx', [(i, i ^ 1) for i in range(lax.axis_size('ctx'...  3.99 us
    pallas_call x4, Pallas kernels, chunk_call(): pl.pallas_call(functools.partial(kernel, steps, kv_here), in_specs=[WHOLE...  3.83 us
    ppermute x2, waiting for transfers between devices, from_section_before(): return lax.ppermute(block, ('section', 'ctx'), route)  2.95 us
    ppermute x2, starting transfers between devices, from_section_before(): return lax.ppermute(block, ('section', 'ctx'), route)  2.77 us
    pallas_call x2, Pallas kernels, first(): pl.pallas_call(functools.partial(first_kernel, other), in_specs=[WHOLE] *...  2.6 us
    ppermute x11, waiting for transfers between devices, swapped(): lax.ppermute(block, 'ctx', [(i, i ^ 1) for i in range(lax.axis_size('ctx'...  1.9 us
  transfers between devices with their start and end apart: 26, of which 13 were waited for; matrix products, arithmetic and copies ran while one was open for 0% of the time, Pallas kernels for 14%

profile of v2, /device:TPU:0, one launch (start us, length us, event | category | flops | bytes accessed | tf_op | source)
XLA Modules:
  0.0 53.5 jit_solution(16894379905025301014)
XLA Ops:
  0.0 1.8 %load_keys.1 = (bf16[784,512]{1,0:T(8,128)(2,1)S(1)}, bf16[784,512]{1,0:T(8,128)(2,1)S(1)}, bf16[24,8192]{1,0:T(8,128)(2,1)S(1)}, f32[1,8192]{1,0:T(1,128)S(1)},...) custom-call(s32[2,24]{1,0:T(2,128)} %act_frames_in.1, ...), custom_call_target="tpu_custom_call" | custom-call | bytes 1572864 | tf_op jit(solution)/shard_map/load_keys/pallas_call | solution.py:278
  1.8 0.5 collective-permute-start
  2.5 0.3 collective-permute-start.1
  2.7 1.3 %first.3 = bf16[4,208,128]{2,1,0:T(8,128)(2,1)S(1)} custom-call(f32[1,8192]{1,0:T(1,128)S(1)} %get-tuple-element.27.gain_ref, f32[2,24,128]{2,1,0:T(8,128)S(1)} %get-tuple-element.20.frames_ref, bf16[24,8192]{1,0:T(8,128)(2,1)S(1)} %get-tuple-element.28.batch_ref, bf16[784,512]{1,0:T(8,128)(2,1)S(1)} %get-tuple-element.23.keys_ref, ...), custom_call_target="tpu_custom_call" | custom-call | flops 452984832 | bytes 1572864 | tf_op jit(solution)/shard_map/first/pallas_call | solution.py:345
  4.0 0.4 collective-permute-start.2
  4.4 1.3 %first.2.mine_ref = bf16[4,208,128]{2,1,0:T(8,128)(2,1)S(1)} custom-call(f32[1,8192]{1,0:T(1,128)S(1)} %get-tuple-element.27.gain_ref, f32[2,24,128]{2,1,0:T(8,128)S(1)} %get-tuple-element.20.frames_ref, bf16[24,8192]{1,0:T(8,128)(2,1)S(1)} %get-tuple-element.28.batch_ref, bf16[784,512]{1,0:T(8,128)(2,1)S(1)} %get-tuple-element.21.keys_ref.refs_0_, ...), custom_call_target="tpu_custom_call" | custom-call | flops 452984832 | bytes 1572864 | tf_op jit(solution)/shard_map/first/pallas_call | solution.py:345
  5.7 0.3 finish.2
  6.1 5.0 %collective-permute-start.3 = (bf16[208,128]{1,0:T(8,128)(2,1)S(1)}, bf16[208,128]{1,0:T(8,128)(2,1)S(1)}, u32[]{:S(2)}, u32[]{:S(2)}) collective-permute-start(bf16[208,128]{1,0:T(8,128)(2,1)S(1)} %get-tuple-element.29), channel_id=1, source_target_pairs={{0,12},{1,13},{2,14},{3,15},{4,8},{5,9},{6,10},{7,11},{8,4},{9,5},... | collective-permute-start | bytes 159752 | tf_op jit(solution)/shard_map/ppermute | solution.py:63
  11.1 0.6 %collective-permute-start.5 = (bf16[208,128]{1,0:T(8,128)(2,1)S(1)}, bf16[208,128]{1,0:T(8,128)(2,1)S(1)}, u32[]{:S(2)}, u32[]{:S(2)}) collective-permute-start(bf16[208,128]{1,0:T(8,128)(2,1)S(1)} %get-tuple-element.31), channel_id=1, source_target_pairs={{0,4},{1,5},{2,6},{3,7},{4,0},{5,1},{6,2},{7,3},{8,12},{9,13},{10,... | collective-permute-start | bytes 159752 | tf_op jit(solution)/shard_map/ppermute | solution.py:63
  11.7 0.2 finish.3.refs_3_
  11.9 1.4 %collective-permute-done.3.refs_0_ = bf16[208,128]{1,0:T(8,128)(2,1)S(1)} collective-permute-done((bf16[208,128]{1,0:T(8,128)(2,1)S(1)}, bf16[208,128]{1,0:T(8,128)(2,1)S(1)}, u32[]{:S(2)}, u32[]{:S(2)}) %collective-permute-start.3) | collective-permute-done | bytes 53280 | tf_op jit(solution)/shard_map/ppermute | solution.py:63
  13.3 2.8 %collective-permute-done.4.refs_1_ = bf16[208,128]{1,0:T(8,128)(2,1)S(1)} collective-permute-done((bf16[208,128]{1,0:T(8,128)(2,1)S(1)}, bf16[208,128]{1,0:T(8,128)(2,1)S(1)}, u32[]{:S(2)}, u32[]{:S(2)}) %collective-permute-start.4) | collective-permute-done | bytes 53280 | tf_op jit(solution)/shard_map/ppermute | solution.py:63
  16.2 0.3 merge.2
  16.5 0.7 %collective-permute-start.6 = (bf16[208,128]{1,0:T(8,128)(2,1)S(1)}, bf16[208,128]{1,0:T(8,128)(2,1)S(1)}, u32[]{:S(2)}, u32[]{:S(2)}) collective-permute-start(bf16[208,128]{1,0:T(8,128)(2,1)S(1)} %merge.2), channel_id=1, source_target_pairs={{0,17},{1,16},{2,19},{3,18},{4,21},{5,20},{6,23},{7,22},{8,25},{9,... | collective-permute-start | bytes 159752 | tf_op jit(solution)/shard_map/ppermute | solution.py:78
  17.2 2.0 %collective-permute-start.7 = (bf16[208,128]{1,0:T(8,128)(2,1)S(1)}, bf16[208,128]{1,0:T(8,128)(2,1)S(1)}, u32[]{:S(2)}, u32[]{:S(2)}) collective-permute-start(bf16[208,128]{1,0:T(8,128)(2,1)S(1)} %merge.2), channel_id=1, source_target_pairs={{0,19},{1,18},{2,17},{3,16},{4,23},{5,22},{6,21},{7,20},{8,27},{9,... | collective-permute-start | bytes 159752 | tf_op jit(solution)/shard_map/ppermute | solution.py:78
  19.2 1.4 %collective-permute-done.6.one_ref = bf16[208,128]{1,0:T(8,128)(2,1)S(1)} collective-permute-done((bf16[208,128]{1,0:T(8,128)(2,1)S(1)}, bf16[208,128]{1,0:T(8,128)(2,1)S(1)}, u32[]{:S(2)}, u32[]{:S(2)}) %collective-permute-start.6) | collective-permute-done | bytes 53280 | tf_op jit(solution)/shard_map/ppermute | solution.py:78
  20.6 1.6 %collective-permute-done.7.two_ref = bf16[208,128]{1,0:T(8,128)(2,1)S(1)} collective-permute-done((bf16[208,128]{1,0:T(8,128)(2,1)S(1)}, bf16[208,128]{1,0:T(8,128)(2,1)S(1)}, u32[]{:S(2)}, u32[]{:S(2)}) %collective-permute-start.7) | collective-permute-done | bytes 53280 | tf_op jit(solution)/shard_map/ppermute | solution.py:78
  22.2 0.3 combine.1
  22.5 2.5 %collective-permute-start.14 = (bf16[192,128]{1,0:T(8,128)(2,1)S(1)}, bf16[192,128]{1,0:T(8,128)(2,1)S(1)}, u32[]{:S(2)}, u32[]{:S(2)}) collective-permute-start(bf16[192,128]{1,0:T(8,128)(2,1)S(1)} %get-tuple-element.33), channel_id=1, source_target_pairs={{0,13},{1,12},{2,15},{3,14},{4,9},{5,8},{6,11},{7,10},{8,5},{9,4},... | collective-permute-start | bytes 147464 | tf_op jit(solution)/shard_map/ppermute | solution.py:63
  25.0 1.8 %collective-permute-start.10 = (bf16[192,128]{1,0:T(8,128)(2,1)S(1)}, bf16[192,128]{1,0:T(8,128)(2,1)S(1)}, u32[]{:S(2)}, u32[]{:S(2)}) collective-permute-start(bf16[192,128]{1,0:T(8,128)(2,1)S(1)} %get-tuple-element.33), channel_id=1, source_target_pairs={{0,5},{1,4},{2,7},{3,6},{4,1},{5,0},{6,3},{7,2},{8,13},{9,12},{10,... | collective-permute-start | bytes 147464 | tf_op jit(solution)/shard_map/ppermute | solution.py:63
  26.7 1.2 %collective-permute-done.14.refs_4_ = bf16[192,128]{1,0:T(8,128)(2,1)S(1)} collective-permute-done((bf16[192,128]{1,0:T(8,128)(2,1)S(1)}, bf16[192,128]{1,0:T(8,128)(2,1)S(1)}, u32[]{:S(2)}, u32[]{:S(2)}) %collective-permute-start.14) | collective-permute-done | bytes 49184 | tf_op jit(solution)/shard_map/ppermute | solution.py:63
  27.9 0.5 %collective-permute-start.8 = (bf16[192,128]{1,0:T(8,128)(2,1)S(1)}, bf16[192,128]{1,0:T(8,128)(2,1)S(1)}, u32[]{:S(2)}, u32[]{:S(2)}) collective-permute-start(bf16[192,128]{1,0:T(8,128)(2,1)S(1)} %get-tuple-element.33), channel_id=1, source_target_pairs={{0,1},{1,0},{2,3},{3,2},{4,5},{5,4},{6,7},{7,6},{8,9},{9,8},{10,11... | collective-permute-start | bytes 147464 | tf_op jit(solution)/shard_map/ppermute | solution.py:52
  28.4 1.0 %partials.7 = bf16[208,128]{1,0:T(8,128)(2,1)S(1)} custom-call(f32[2,24,128]{2,1,0:T(8,128)S(1)} %get-tuple-element.20.frames_ref, bf16[784,512]{1,0:T(8,128)(2,1)S(1)} %get-tuple-element.21.keys_ref.refs_0_, bf16[768,512]{1,0:T(8,128)(2,1)S(1)} %get-tuple-element.22.values_ref.refs_1_, bf16[784,512]{1,0:T(8,128)(2,1)S(1)} %collective-permute-done.refs_2_, ...), custom_call_target="tpu_custom_call" | custom-call | flops 226492416 | bytes 786432 | tf_op jit(solution)/shard_map/partials/pallas_call | solution.py:387
  29.4 2.5 %collective-permute-start.15 = (bf16[208,128]{1,0:T(8,128)(2,1)S(1)}, bf16[208,128]{1,0:T(8,128)(2,1)S(1)}, u32[]{:S(2)}, u32[]{:S(2)}) collective-permute-start(bf16[208,128]{1,0:T(8,128)(2,1)S(1)} %partials.7), channel_id=1, source_target_pairs={{0,13},{1,12},{2,15},{3,14},{4,9},{5,8},{6,11},{7,10},{8,5},{9,4},... | collective-permute-start | bytes 159752 | tf_op jit(solution)/shard_map/ppermute | solution.py:63
  31.9 0.9 %partials.6 = bf16[208,128]{1,0:T(8,128)(2,1)S(1)} custom-call(f32[2,24,128]{2,1,0:T(8,128)S(1)} %get-tuple-element.20.frames_ref, bf16[784,512]{1,0:T(8,128)(2,1)S(1)} %get-tuple-element.21.keys_ref.refs_0_, bf16[768,512]{1,0:T(8,128)(2,1)S(1)} %get-tuple-element.22.values_ref.refs_1_, bf16[784,512]{1,0:T(8,128)(2,1)S(1)} %collective-permute-done.refs_2_, ...), custom_call_target="tpu_custom_call" | custom-call | flops 226492416 | bytes 786432 | tf_op jit(solution)/shard_map/partials/pallas_call | solution.py:387
  32.9 1.0 %partials.5 = bf16[208,128]{1,0:T(8,128)(2,1)S(1)} custom-call(f32[2,24,128]{2,1,0:T(8,128)S(1)} %get-tuple-element.20.frames_ref, bf16[784,512]{1,0:T(8,128)(2,1)S(1)} %get-tuple-element.21.keys_ref.refs_0_, bf16[768,512]{1,0:T(8,128)(2,1)S(1)} %get-tuple-element.22.values_ref.refs_1_, bf16[784,512]{1,0:T(8,128)(2,1)S(1)} %collective-permute-done.refs_2_, ...), custom_call_target="tpu_custom_call" | custom-call | flops 226492416 | bytes 786432 | tf_op jit(solution)/shard_map/partials/pallas_call | solution.py:387
  33.9 1.4 %collective-permute-start.11 = (bf16[208,128]{1,0:T(8,128)(2,1)S(1)}, bf16[208,128]{1,0:T(8,128)(2,1)S(1)}, u32[]{:S(2)}, u32[]{:S(2)}) collective-permute-start(bf16[208,128]{1,0:T(8,128)(2,1)S(1)} %partials.5), channel_id=1, source_target_pairs={{0,5},{1,4},{2,7},{3,6},{4,1},{5,0},{6,3},{7,2},{8,13},{9,12},{10,... | collective-permute-start | bytes 159752 | tf_op jit(solution)/shard_map/ppermute | solution.py:63
  35.3 1.0 %partials.4 = bf16[208,128]{1,0:T(8,128)(2,1)S(1)} custom-call(f32[2,24,128]{2,1,0:T(8,128)S(1)} %get-tuple-element.20.frames_ref, bf16[784,512]{1,0:T(8,128)(2,1)S(1)} %get-tuple-element.21.keys_ref.refs_0_, bf16[768,512]{1,0:T(8,128)(2,1)S(1)} %get-tuple-element.22.values_ref.refs_1_, bf16[784,512]{1,0:T(8,128)(2,1)S(1)} %collective-permute-done.refs_2_, ...), custom_call_target="tpu_custom_call" | custom-call | flops 226492416 | bytes 786432 | tf_op jit(solution)/shard_map/partials/pallas_call | solution.py:387
  36.2 0.5 %collective-permute-start.9 = (bf16[208,128]{1,0:T(8,128)(2,1)S(1)}, bf16[208,128]{1,0:T(8,128)(2,1)S(1)}, u32[]{:S(2)}, u32[]{:S(2)}) collective-permute-start(bf16[208,128]{1,0:T(8,128)(2,1)S(1)} %partials.4), channel_id=1, source_target_pairs={{0,1},{1,0},{2,3},{3,2},{4,5},{5,4},{6,7},{7,6},{8,9},{9,8},{10,11... | collective-permute-start | bytes 159752 | tf_op jit(solution)/shard_map/ppermute | solution.py:52
  36.8 0.6 %collective-permute-done.13.refs_2_ = bf16[208,128]{1,0:T(8,128)(2,1)S(1)} collective-permute-done((bf16[208,128]{1,0:T(8,128)(2,1)S(1)}, bf16[208,128]{1,0:T(8,128)(2,1)S(1)}, u32[]{:S(2)}, u32[]{:S(2)}) %collective-permute-start.13) | collective-permute-done | bytes 53280 | tf_op jit(solution)/shard_map/ppermute | solution.py:63
  37.4 1.5 %collective-permute-done.11.refs_1_ = bf16[208,128]{1,0:T(8,128)(2,1)S(1)} collective-permute-done((bf16[208,128]{1,0:T(8,128)(2,1)S(1)}, bf16[208,128]{1,0:T(8,128)(2,1)S(1)}, u32[]{:S(2)}, u32[]{:S(2)}) %collective-permute-start.11) | collective-permute-done | bytes 53280 | tf_op jit(solution)/shard_map/ppermute | solution.py:63
  39.0 0.3 merge.3
  39.2 1.0 %collective-permute-start.16 = (bf16[208,128]{1,0:T(8,128)(2,1)S(1)}, bf16[208,128]{1,0:T(8,128)(2,1)S(1)}, u32[]{:S(2)}, u32[]{:S(2)}) collective-permute-start(bf16[208,128]{1,0:T(8,128)(2,1)S(1)} %merge.3), channel_id=1, source_target_pairs={{0,3},{1,2},{2,1},{3,0},{4,7},{5,6},{6,5},{7,4},{8,11},{9,10},{10,... | collective-permute-start | bytes 159752 | tf_op jit(solution)/shard_map/ppermute | solution.py:57
  40.3 0.3 collective-permute-start.17
  40.5 0.2 collective-permute-start.18
  40.8 1.0 %collective-permute-done.18.share_ref = bf16[24,1024]{1,0:T(8,128)(2,1)S(1)} collective-permute-done((bf16[24,1024]{1,0:T(8,128)(2,1)S(1)}, bf16[24,1024]{1,0:T(8,128)(2,1)S(1)}, u32[]{:S(2)}, u32[]{:S(2)}) %collective-permute-start.18) | collective-permute-done | bytes 49184 | tf_op jit(solution)/shard_map/ppermute | solution.py:52
  41.8 1.3 %collective-permute-done.16.two_ref = bf16[208,128]{1,0:T(8,128)(2,1)S(1)} collective-permute-done((bf16[208,128]{1,0:T(8,128)(2,1)S(1)}, bf16[208,128]{1,0:T(8,128)(2,1)S(1)}, u32[]{:S(2)}, u32[]{:S(2)}) %collective-permute-start.16) | collective-permute-done | bytes 53280 | tf_op jit(solution)/shard_map/ppermute | solution.py:57
  43.1 0.2 combine_last.1.refs_3_
  43.4 2.0 %collective-permute-start.19 = (bf16[24,1024]{1,0:T(8,128)(2,1)S(1)}, bf16[24,1024]{1,0:T(8,128)(2,1)S(1)}, u32[]{:S(2)}, u32[]{:S(2)}) collective-permute-start(bf16[24,1024]{1,0:T(8,128)(2,1)S(1)} %combine_last.1.refs_3_), channel_id=1, source_target_pairs={{0,13},{1,12},{2,15},{3,14},{4,9},{5,8},{6,11},{7,10},{8,5},{9,4},... | collective-permute-start | bytes 147464 | tf_op jit(solution)/shard_map/ppermute | solution.py:63
  45.4 1.9 %collective-permute-start.23 = (bf16[24,1024]{1,0:T(8,128)(2,1)S(1)}, bf16[24,1024]{1,0:T(8,128)(2,1)S(1)}, u32[]{:S(2)}, u32[]{:S(2)}) collective-permute-start(bf16[24,1024]{1,0:T(8,128)(2,1)S(1)} %combine_last.1.refs_3_), channel_id=1, source_target_pairs={{0,5},{1,4},{2,7},{3,6},{4,1},{5,0},{6,3},{7,2},{8,13},{9,12},{10,... | collective-permute-start | bytes 147464 | tf_op jit(solution)/shard_map/ppermute | solution.py:63
  47.3 0.4 collective-permute-start.25
  47.7 1.4 %collective-permute-done.19.refs_4_ = bf16[24,1024]{1,0:T(8,128)(2,1)S(1)} collective-permute-done((bf16[24,1024]{1,0:T(8,128)(2,1)S(1)}, bf16[24,1024]{1,0:T(8,128)(2,1)S(1)}, u32[]{:S(2)}, u32[]{:S(2)}) %collective-permute-start.19) | collective-permute-done | bytes 49184 | tf_op jit(solution)/shard_map/ppermute | solution.py:63
  49.0 0.4 collective-permute-start.20
  49.4 1.9 %collective-permute-done.21.refs_5_ = bf16[24,1024]{1,0:T(8,128)(2,1)S(1)} collective-permute-done((bf16[24,1024]{1,0:T(8,128)(2,1)S(1)}, bf16[24,1024]{1,0:T(8,128)(2,1)S(1)}, u32[]{:S(2)}, u32[]{:S(2)}) %collective-permute-start.21) | collective-permute-done | bytes 49184 | tf_op jit(solution)/shard_map/ppermute | solution.py:63
  51.4 0.4 collective-permute-start.24
  51.8 0.7 %collective-permute-done.22.refs_1_ = bf16[24,1024]{1,0:T(8,128)(2,1)S(1)} collective-permute-done((bf16[24,1024]{1,0:T(8,128)(2,1)S(1)}, bf16[24,1024]{1,0:T(8,128)(2,1)S(1)}, u32[]{:S(2)}, u32[]{:S(2)}) %collective-permute-start.22) | collective-permute-done | bytes 49184 | tf_op jit(solution)/shard_map/ppermute | solution.py:52
  52.6 0.2 collective-permute-done.24.refs_2_
  52.7 0.8 %assemble.1 = bf16[24,8192]{1,0:T(8,128)(2,1)} custom-call(bf16[24,1024]{1,0:T(8,128)(2,1)S(1)} %collective-permute-done.20.refs_0_, bf16[24,1024]{1,0:T(8,128)(2,1)S(1)} %collective-permute-done.22.refs_1_, bf16[24,1024]{1,0:T(8,128)(2,1)S(1)} %collective-permute-done.24.refs_2_, bf16[24,1024]{1,0:T(8,128)(2,1)S(1)} %combine_last.1.refs_3_, ...), custom_call_target="tpu_custom_call" | custom-call | tf_op jit(solution)/shard_map/assemble/pallas_call | solution.py:518
  (21 shorter events, 0.3 us)
Async XLA Ops:
  0.0 2.4 %copy-start = (bf16[1,768,1024]{2,1,0:T(8,128)(2,1)S(1)}, bf16[1,768,1024]{2,1,0:T(8,128)(2,1)}, u32[]{:S(2)}) copy-start(bf16[1,768,1024]{2,1,0:T(8,128)(2,1)} %param.14) | copy-start | bytes 4718596
  1.8 26.6 %collective-permute-start = (bf16[784,512]{1,0:T(8,128)(2,1)S(1)}, bf16[784,512]{1,0:T(8,128)(2,1)S(1)}, u32[]{:S(2)}, u32[]{:S(2)}) collective-permute-start(bf16[784,512]{1,0:T(8,128)(2,1)S(1)} %get-tuple-element.23.keys_ref), channel_id=1, source_target_pairs={{0,1},{1,0},{2,3},{3,2},{4,5},{5,4},{6,7},{7,6},{8,9},{9,8},{10,11... | collective-permute-start | bytes 2408456 | tf_op jit(solution)/shard_map/ppermute | solution.py:52
  2.5 26.0 %collective-permute-start.1 = (bf16[768,512]{1,0:T(8,128)(2,1)S(1)}, bf16[768,512]{1,0:T(8,128)(2,1)S(1)}, u32[]{:S(2)}, u32[]{:S(2)}) collective-permute-start(bf16[768,512]{1,0:T(8,128)(2,1)S(1)} %get-tuple-element.24.values_ref), channel_id=1, source_target_pairs={{0,1},{1,0},{2,3},{3,2},{4,5},{5,4},{6,7},{7,6},{8,9},{9,8},{10,11... | collective-permute-start | bytes 2359304 | tf_op jit(solution)/shard_map/ppermute | solution.py:52
  4.0 1.7 %collective-permute-start.2 = (bf16[4,208,128]{2,1,0:T(8,128)(2,1)S(1)}, bf16[4,208,128]{2,1,0:T(8,128)(2,1)S(1)}, u32[]{:S(2)}, u32[]{:S(2)}) collective-permute-start(bf16[4,208,128]{2,1,0:T(8,128)(2,1)S(1)} %first.3), channel_id=1, source_target_pairs={{0,1},{1,0},{2,3},{3,2},{4,5},{5,4},{6,7},{7,6},{8,9},{9,8},{10,11... | collective-permute-start | bytes 638984 | tf_op jit(solution)/shard_map/ppermute | solution.py:52
  6.1 7.3 %collective-permute-start.3 = (bf16[208,128]{1,0:T(8,128)(2,1)S(1)}, bf16[208,128]{1,0:T(8,128)(2,1)S(1)}, u32[]{:S(2)}, u32[]{:S(2)}) collective-permute-start(bf16[208,128]{1,0:T(8,128)(2,1)S(1)} %get-tuple-element.29), channel_id=1, source_target_pairs={{0,12},{1,13},{2,14},{3,15},{4,8},{5,9},{6,10},{7,11},{8,4},{9,5},... | collective-permute-start | bytes 159752 | tf_op jit(solution)/shard_map/ppermute | solution.py:63
  11.1 5.1 %collective-permute-start.4 = (bf16[208,128]{1,0:T(8,128)(2,1)S(1)}, bf16[208,128]{1,0:T(8,128)(2,1)S(1)}, u32[]{:S(2)}, u32[]{:S(2)}) collective-permute-start(bf16[208,128]{1,0:T(8,128)(2,1)S(1)} %get-tuple-element.30), channel_id=1, source_target_pairs={{0,8},{1,9},{2,10},{3,11},{4,12},{5,13},{6,14},{7,15},{8,0},{9,1},... | collective-permute-start | bytes 159752 | tf_op jit(solution)/shard_map/ppermute | solution.py:63
  11.1 5.1 %collective-permute-start.5 = (bf16[208,128]{1,0:T(8,128)(2,1)S(1)}, bf16[208,128]{1,0:T(8,128)(2,1)S(1)}, u32[]{:S(2)}, u32[]{:S(2)}) collective-permute-start(bf16[208,128]{1,0:T(8,128)(2,1)S(1)} %get-tuple-element.31), channel_id=1, source_target_pairs={{0,4},{1,5},{2,6},{3,7},{4,0},{5,1},{6,2},{7,3},{8,12},{9,13},{10,... | collective-permute-start | bytes 159752 | tf_op jit(solution)/shard_map/ppermute | solution.py:63
  16.5 4.1 %collective-permute-start.6 = (bf16[208,128]{1,0:T(8,128)(2,1)S(1)}, bf16[208,128]{1,0:T(8,128)(2,1)S(1)}, u32[]{:S(2)}, u32[]{:S(2)}) collective-permute-start(bf16[208,128]{1,0:T(8,128)(2,1)S(1)} %merge.2), channel_id=1, source_target_pairs={{0,17},{1,16},{2,19},{3,18},{4,21},{5,20},{6,23},{7,22},{8,25},{9,... | collective-permute-start | bytes 159752 | tf_op jit(solution)/shard_map/ppermute | solution.py:78
  17.2 5.0 %collective-permute-start.7 = (bf16[208,128]{1,0:T(8,128)(2,1)S(1)}, bf16[208,128]{1,0:T(8,128)(2,1)S(1)}, u32[]{:S(2)}, u32[]{:S(2)}) collective-permute-start(bf16[208,128]{1,0:T(8,128)(2,1)S(1)} %merge.2), channel_id=1, source_target_pairs={{0,19},{1,18},{2,17},{3,16},{4,23},{5,22},{6,21},{7,20},{8,27},{9,... | collective-permute-start | bytes 159752 | tf_op jit(solution)/shard_map/ppermute | solution.py:78
  22.5 5.4 %collective-permute-start.14 = (bf16[192,128]{1,0:T(8,128)(2,1)S(1)}, bf16[192,128]{1,0:T(8,128)(2,1)S(1)}, u32[]{:S(2)}, u32[]{:S(2)}) collective-permute-start(bf16[192,128]{1,0:T(8,128)(2,1)S(1)} %get-tuple-element.33), channel_id=1, source_target_pairs={{0,13},{1,12},{2,15},{3,14},{4,9},{5,8},{6,11},{7,10},{8,5},{9,4},... | collective-permute-start | bytes 147464 | tf_op jit(solution)/shard_map/ppermute | solution.py:63
  25.0 6.9 %collective-permute-start.12 = (bf16[192,128]{1,0:T(8,128)(2,1)S(1)}, bf16[192,128]{1,0:T(8,128)(2,1)S(1)}, u32[]{:S(2)}, u32[]{:S(2)}) collective-permute-start(bf16[192,128]{1,0:T(8,128)(2,1)S(1)} %get-tuple-element.33), channel_id=1, source_target_pairs={{0,9},{1,8},{2,11},{3,10},{4,13},{5,12},{6,15},{7,14},{8,1},{9,0},... | collective-permute-start | bytes 147464 | tf_op jit(solution)/shard_map/ppermute | solution.py:63
  25.0 7.9 %collective-permute-start.10 = (bf16[192,128]{1,0:T(8,128)(2,1)S(1)}, bf16[192,128]{1,0:T(8,128)(2,1)S(1)}, u32[]{:S(2)}, u32[]{:S(2)}) collective-permute-start(bf16[192,128]{1,0:T(8,128)(2,1)S(1)} %get-tuple-element.33), channel_id=1, source_target_pairs={{0,5},{1,4},{2,7},{3,6},{4,1},{5,0},{6,3},{7,2},{8,13},{9,12},{10,... | collective-permute-start | bytes 147464 | tf_op jit(solution)/shard_map/ppermute | solution.py:63
  27.9 7.4 %collective-permute-start.8 = (bf16[192,128]{1,0:T(8,128)(2,1)S(1)}, bf16[192,128]{1,0:T(8,128)(2,1)S(1)}, u32[]{:S(2)}, u32[]{:S(2)}) collective-permute-start(bf16[192,128]{1,0:T(8,128)(2,1)S(1)} %get-tuple-element.33), channel_id=1, source_target_pairs={{0,1},{1,0},{2,3},{3,2},{4,5},{5,4},{6,7},{7,6},{8,9},{9,8},{10,11... | collective-permute-start | bytes 147464 | tf_op jit(solution)/shard_map/ppermute | solution.py:52
  29.4 7.4 %collective-permute-start.15 = (bf16[208,128]{1,0:T(8,128)(2,1)S(1)}, bf16[208,128]{1,0:T(8,128)(2,1)S(1)}, u32[]{:S(2)}, u32[]{:S(2)}) collective-permute-start(bf16[208,128]{1,0:T(8,128)(2,1)S(1)} %partials.7), channel_id=1, source_target_pairs={{0,13},{1,12},{2,15},{3,14},{4,9},{5,8},{6,11},{7,10},{8,5},{9,4},... | collective-permute-start | bytes 159752 | tf_op jit(solution)/shard_map/ppermute | solution.py:63
  32.8 4.6 %collective-permute-start.13 = (bf16[208,128]{1,0:T(8,128)(2,1)S(1)}, bf16[208,128]{1,0:T(8,128)(2,1)S(1)}, u32[]{:S(2)}, u32[]{:S(2)}) collective-permute-start(bf16[208,128]{1,0:T(8,128)(2,1)S(1)} %partials.6), channel_id=1, source_target_pairs={{0,9},{1,8},{2,11},{3,10},{4,13},{5,12},{6,15},{7,14},{8,1},{9,0},... | collective-permute-start | bytes 159752 | tf_op jit(solution)/shard_map/ppermute | solution.py:63
  33.9 5.1 %collective-permute-start.11 = (bf16[208,128]{1,0:T(8,128)(2,1)S(1)}, bf16[208,128]{1,0:T(8,128)(2,1)S(1)}, u32[]{:S(2)}, u32[]{:S(2)}) collective-permute-start(bf16[208,128]{1,0:T(8,128)(2,1)S(1)} %partials.5), channel_id=1, source_target_pairs={{0,5},{1,4},{2,7},{3,6},{4,1},{5,0},{6,3},{7,2},{8,13},{9,12},{10,... | collective-permute-start | bytes 159752 | tf_op jit(solution)/shard_map/ppermute | solution.py:63
  36.2 2.7 %collective-permute-start.9 = (bf16[208,128]{1,0:T(8,128)(2,1)S(1)}, bf16[208,128]{1,0:T(8,128)(2,1)S(1)}, u32[]{:S(2)}, u32[]{:S(2)}) collective-permute-start(bf16[208,128]{1,0:T(8,128)(2,1)S(1)} %partials.4), channel_id=1, source_target_pairs={{0,1},{1,0},{2,3},{3,2},{4,5},{5,4},{6,7},{7,6},{8,9},{9,8},{10,11... | collective-permute-start | bytes 159752 | tf_op jit(solution)/shard_map/ppermute | solution.py:52
  39.2 3.9 %collective-permute-start.16 = (bf16[208,128]{1,0:T(8,128)(2,1)S(1)}, bf16[208,128]{1,0:T(8,128)(2,1)S(1)}, u32[]{:S(2)}, u32[]{:S(2)}) collective-permute-start(bf16[208,128]{1,0:T(8,128)(2,1)S(1)} %merge.3), channel_id=1, source_target_pairs={{0,3},{1,2},{2,1},{3,0},{4,7},{5,6},{6,5},{7,4},{8,11},{9,10},{10,... | collective-permute-start | bytes 159752 | tf_op jit(solution)/shard_map/ppermute | solution.py:57
  40.3 2.9 %collective-permute-start.17 = (bf16[208,128]{1,0:T(8,128)(2,1)S(1)}, bf16[208,128]{1,0:T(8,128)(2,1)S(1)}, u32[]{:S(2)}, u32[]{:S(2)}) collective-permute-start(bf16[208,128]{1,0:T(8,128)(2,1)S(1)} %merge.3), channel_id=1, source_target_pairs={{0,1},{1,0},{2,3},{3,2},{4,5},{5,4},{6,7},{7,6},{8,9},{9,8},{10,11... | collective-permute-start | bytes 159752 | tf_op jit(solution)/shard_map/ppermute | solution.py:52
  40.5 1.2 %collective-permute-start.18 = (bf16[24,1024]{1,0:T(8,128)(2,1)S(1)}, bf16[24,1024]{1,0:T(8,128)(2,1)S(1)}, u32[]{:S(2)}, u32[]{:S(2)}) collective-permute-start(bf16[24,1024]{1,0:T(8,128)(2,1)S(1)} %get-tuple-element.34), channel_id=1, source_target_pairs={{0,1},{1,0},{2,3},{3,2},{4,5},{5,4},{6,7},{7,6},{8,9},{9,8},{10,11... | collective-permute-start | bytes 147464 | tf_op jit(solution)/shard_map/ppermute | solution.py:52
  43.4 5.7 %collective-permute-start.19 = (bf16[24,1024]{1,0:T(8,128)(2,1)S(1)}, bf16[24,1024]{1,0:T(8,128)(2,1)S(1)}, u32[]{:S(2)}, u32[]{:S(2)}) collective-permute-start(bf16[24,1024]{1,0:T(8,128)(2,1)S(1)} %combine_last.1.refs_3_), channel_id=1, source_target_pairs={{0,13},{1,12},{2,15},{3,14},{4,9},{5,8},{6,11},{7,10},{8,5},{9,4},... | collective-permute-start | bytes 147464 | tf_op jit(solution)/shard_map/ppermute | solution.py:63
  45.4 5.9 %collective-permute-start.21 = (bf16[24,1024]{1,0:T(8,128)(2,1)S(1)}, bf16[24,1024]{1,0:T(8,128)(2,1)S(1)}, u32[]{:S(2)}, u32[]{:S(2)}) collective-permute-start(bf16[24,1024]{1,0:T(8,128)(2,1)S(1)} %combine_last.1.refs_3_), channel_id=1, source_target_pairs={{0,9},{1,8},{2,11},{3,10},{4,13},{5,12},{6,15},{7,14},{8,1},{9,0},... | collective-permute-start | bytes 147464 | tf_op jit(solution)/shard_map/ppermute | solution.py:63
  45.4 6.0 %collective-permute-start.23 = (bf16[24,1024]{1,0:T(8,128)(2,1)S(1)}, bf16[24,1024]{1,0:T(8,128)(2,1)S(1)}, u32[]{:S(2)}, u32[]{:S(2)}) collective-permute-start(bf16[24,1024]{1,0:T(8,128)(2,1)S(1)} %combine_last.1.refs_3_), channel_id=1, source_target_pairs={{0,5},{1,4},{2,7},{3,6},{4,1},{5,0},{6,3},{7,2},{8,13},{9,12},{10,... | collective-permute-start | bytes 147464 | tf_op jit(solution)/shard_map/ppermute | solution.py:63
  47.3 4.6 %collective-permute-start.25 = (bf16[24,1024]{1,0:T(8,128)(2,1)S(1)}, bf16[24,1024]{1,0:T(8,128)(2,1)S(1)}, u32[]{:S(2)}, u32[]{:S(2)}) collective-permute-start(bf16[24,1024]{1,0:T(8,128)(2,1)S(1)} %combine_last.1.refs_3_), channel_id=1, source_target_pairs={{0,1},{1,0},{2,3},{3,2},{4,5},{5,4},{6,7},{7,6},{8,9},{9,8},{10,11... | collective-permute-start | bytes 147464 | tf_op jit(solution)/shard_map/ppermute | solution.py:52
  49.0 2.8 %collective-permute-start.20 = (bf16[24,1024]{1,0:T(8,128)(2,1)S(1)}, bf16[24,1024]{1,0:T(8,128)(2,1)S(1)}, u32[]{:S(2)}, u32[]{:S(2)}) collective-permute-start(bf16[24,1024]{1,0:T(8,128)(2,1)S(1)} %collective-permute-done.19.refs_4_), channel_id=1, source_target_pairs={{0,1},{1,0},{2,3},{3,2},{4,5},{5,4},{6,7},{7,6},{8,9},{9,8},{10,11... | collective-permute-start | bytes 147464 | tf_op jit(solution)/shard_map/ppermute | solution.py:52
  51.3 1.2 %collective-permute-start.22 = (bf16[24,1024]{1,0:T(8,128)(2,1)S(1)}, bf16[24,1024]{1,0:T(8,128)(2,1)S(1)}, u32[]{:S(2)}, u32[]{:S(2)}) collective-permute-start(bf16[24,1024]{1,0:T(8,128)(2,1)S(1)} %collective-permute-done.21.refs_5_), channel_id=1, source_target_pairs={{0,1},{1,0},{2,3},{3,2},{4,5},{5,4},{6,7},{7,6},{8,9},{9,8},{10,11... | collective-permute-start | bytes 147464 | tf_op jit(solution)/shard_map/ppermute | solution.py:52
  51.4 1.3 %collective-permute-start.24 = (bf16[24,1024]{1,0:T(8,128)(2,1)S(1)}, bf16[24,1024]{1,0:T(8,128)(2,1)S(1)}, u32[]{:S(2)}, u32[]{:S(2)}) collective-permute-start(bf16[24,1024]{1,0:T(8,128)(2,1)S(1)} %collective-permute-done.23.refs_6_), channel_id=1, source_target_pairs={{0,1},{1,0},{2,3},{3,2},{4,5},{5,4},{6,7},{7,6},{8,9},{9,8},{10,11... | collective-permute-start | bytes 147464 | tf_op jit(solution)/shard_map/ppermute | solution.py:52
